TPU v7x, 256 devices: a whole 4x4x8 slice. The times are simulated.
256 devices in a mesh: row: 16 (over z_hi, x), col: 8 (over y, z_lo), feat: 2 (over core).
Axes of the slice: x: 4, y: 4, z: 8 (z_hi: 4, z_lo: 2; z = z_hi * 2 + z_lo), core: 2. Of those that a mesh axis runs over, the one named last changes fastest.
Arguments:
- tile_vals: bfloat16 [16, 8, 384, 128, 128], P('row', 'col'), may hold values from -0.09375 to 0.09375
- tile_rows: int32 [16, 8, 384], P('row', 'col'), may hold values from 0 to 31, as said below
- tile_cols: int32 [16, 8, 384], P('row', 'col'), may hold values from 0 to 63, as said below
- tile_count: int32 [16, 8], P('row', 'col'), may hold values from 1 to 384, as said below
- features: bfloat16 [65536, 256], P(('row', 'col'), 'feat'), may hold values from -6 to 6
- weight: bfloat16 [256, 256], P(None, 'feat'), may hold values from -0.375 to 0.375
- bias_term: float32 [256], P('feat'), may hold values from -3 to 3
- cotangent: bfloat16 [65536, 256], P(('row', 'col'), 'feat'), may hold values from -6 to 6
Outputs:
- outputs: bfloat16 [65536, 256], P(('row', 'col'), 'feat')
- grad_feat: bfloat16 [65536, 256], P(('row', 'col'), 'feat')
- grad_weight: float32 [256, 256], P(None, 'feat')
- grad_bias: float32 [256], P('feat')
Inputs may be any that keep to these rules, and one draw needn't show every extreme that they name: Within one grid cell the live slots name distinct tile positions; tile_rows is below 32. tile_cols is below 64; the position of a slot is tile_rows * 64 + tile_cols. `tile_count`: some grid cell has all 384 slots live in every draw.
All inputs are finite; a program needn't handle non-finite values.
Results may differ from a plain program's by a relative error of at most 0.025.
Values may be sent and summed in bfloat16 or wider, within the bound.
No kernel may reach another device: no remote copies, remote signals or barrier semaphores. Data moves between devices by JAX's collectives and lax.ppermute only.
A program may use at most 128 MiB of HBM per device.

v0:
```python
import functools
import math

import jax
import jax.numpy as jnp
from jax import lax
from jax.experimental import pallas as pl
from jax.experimental.pallas import tpu as pltpu
from jax.sharding import Mesh
from jax.sharding import PartitionSpec as P

BF16 = jnp.bfloat16
F32 = jnp.float32
EDGE = 128
CHUNK = 32
DEPTH = 3
HALF_TILES = 32
VMEM_LIMIT = 40 * 2**20


def pull(value, axis, size, step):
    return lax.ppermute(value, axis, [((i + step) % size, i) for i in range(size)])


def push(value, axis, size, step):
    return lax.ppermute(value, axis, [(i, (i + step) % size) for i in range(size)])


def push_col(value, step_y, step_z):
    pairs = []
    for y in range(4):
        for z in range(2):
            pairs.append((y * 2 + z, ((y + step_y) % 4) * 2 + (z + step_z) % 2))
    return lax.ppermute(value, ("y", "zlo"), pairs)


def slot_lists(rows, cols, second, live):
    slots = rows.shape[0]
    index = jnp.arange(slots, dtype=jnp.int32)
    code = index * 4096 + rows * 64 + cols
    kind = jnp.stack([jnp.logical_not(second), second]) & (index < live)[None]
    before = index[None, :] < index[:, None]
    rank = jnp.sum((kind[:, None, :] & before[None]).astype(jnp.int32), axis=2)
    hit = kind[:, None, :] & (rank[:, None, :] == index[None, :, None])
    packed = jnp.sum(jnp.where(hit, code[None, None, :], 0), axis=2)
    totals = jnp.sum(kind.astype(jnp.int32), axis=1)
    packed = jnp.where(index[None] < totals[:, None], packed, 32 * 64 + 32)
    return packed, totals


def tile_kernel(transpose, n_src, n_out, has_base, total_ref, list_ref, tiles_hbm, *refs):
    src_refs = refs[:n_src]
    base = refs[n_src] if has_base else None
    n_in = n_src + has_base
    out_refs = refs[n_in : n_in + n_out]
    buf, sem, source, acc = refs[n_in + n_out :]
    chunks = (total_ref[0] + CHUNK - 1) // CHUNK

    def fetch(index):
        slot = lax.rem(index, DEPTH)
        for k in range(CHUNK):
            code = list_ref[index * CHUNK + k]
            pltpu.make_async_copy(
                tiles_hbm.at[lax.shift_right_logical(code, 12)], buf.at[slot, k], sem.at[slot]
            ).start()

    for k in range(DEPTH - 1):

        @pl.when(k < chunks)
        def _():
            fetch(jnp.int32(k))

    per = src_refs[0].shape[0] // EDGE
    for k in range(n_src):
        source[k * per : (k + 1) * per] = src_refs[k][...].reshape(per, EDGE, EDGE)
    source[n_src * per] = jnp.zeros((EDGE, EDGE), BF16)
    acc[...] = jnp.zeros_like(acc)

    def one_chunk(index, carry):
        slot = lax.rem(index, DEPTH)

        @pl.when(index + DEPTH - 1 < chunks)
        def _():
            fetch(index + DEPTH - 1)

        pltpu.make_async_copy(tiles_hbm.at[pl.ds(0, CHUNK)], buf.at[slot], sem.at[slot]).wait()
        for k in range(CHUNK):
            code = list_ref[index * CHUNK + k]
            row_at = lax.shift_right_logical(code, 6) & 63
            col_at = code & 63
            out_at, src_at = (col_at, row_at) if transpose else (row_at, col_at)
            dims = (((0,), (0,)), ((), ())) if transpose else (((1,), (0,)), ((), ()))
            acc[out_at] += lax.dot_general(
                buf[slot, k], source[src_at], dims, preferred_element_type=F32
            )
        return carry

    lax.fori_loop(0, chunks, one_chunk, 0)
    if out_refs[0].dtype == F32:
        out_refs[0][...] = acc[0:HALF_TILES]
        return
    per = out_refs[0].shape[0] // EDGE
    for k in range(n_out):
        total = acc[k * per : (k + 1) * per]
        if has_base:
            total = total + base[k * per : (k + 1) * per]
        out_refs[k][...] = total.reshape(per * EDGE, EDGE).astype(BF16)


def tile_pass(tiles, packed, total, sources, base, out_shape, transpose, name):
    smem = pl.BlockSpec(memory_space=pltpu.SMEM)
    vmem = pl.BlockSpec(memory_space=pltpu.VMEM)
    inputs = list(sources) + ([] if base is None else [base])
    return pl.pallas_call(
        functools.partial(
            tile_kernel, transpose, len(sources), len(out_shape), int(base is not None)
        ),
        out_shape=out_shape,
        in_specs=[smem, smem, pl.BlockSpec(memory_space=pl.ANY)] + [vmem] * len(inputs),
        out_specs=[vmem] * len(out_shape),
        scratch_shapes=[
            pltpu.VMEM((DEPTH, CHUNK, EDGE, EDGE), BF16),
            pltpu.SemaphoreType.DMA((DEPTH,)),
            pltpu.VMEM((HALF_TILES + 1, EDGE, EDGE), BF16),
            pltpu.VMEM((HALF_TILES + 1, EDGE, EDGE), F32),
        ],
        compiler_params=pltpu.CompilerParams(vmem_limit_bytes=VMEM_LIMIT),
        cost_estimate=pl.CostEstimate(
            flops=2 * tiles.size * EDGE, bytes_accessed=2 * tiles.size, transcendentals=0
        ),
        name=name,
    )(total, packed, tiles, *inputs)


def sum_kernel(*refs):
    total = refs[0][...].astype(F32)
    for ref in refs[1:-1]:
        total = total + ref[...].astype(F32)
    refs[-1][...] = total.astype(refs[-1].dtype)


def sum_blocks(blocks, dtype, name):
    vmem = pl.BlockSpec(memory_space=pltpu.VMEM)
    return pl.pallas_call(
        sum_kernel,
        out_shape=jax.ShapeDtypeStruct(blocks[0].shape, dtype),
        in_specs=[vmem] * len(blocks),
        out_specs=vmem,
        compiler_params=pltpu.CompilerParams(vmem_limit_bytes=VMEM_LIMIT),
        name=name,
    )(*blocks)


def sum_pair_kernel(*refs):
    total = refs[0][...].astype(F32)
    for ref in refs[1:-2]:
        total = total + ref[...].astype(F32)
    rows = refs[-1].shape[0]
    refs[-2][...] = total[:rows].astype(refs[-2].dtype)
    refs[-1][...] = total[rows:].astype(refs[-1].dtype)


def sum_pair(blocks, dtypes, name):
    vmem = pl.BlockSpec(memory_space=pltpu.VMEM)
    rows, width = blocks[0].shape
    return pl.pallas_call(
        sum_pair_kernel,
        out_shape=[jax.ShapeDtypeStruct((rows // 2, width), d) for d in dtypes],
        in_specs=[vmem] * len(blocks),
        out_specs=[vmem] * 2,
        compiler_params=pltpu.CompilerParams(vmem_limit_bytes=VMEM_LIMIT),
        name=name,
    )(*blocks)


def middle_kernel(
    scale, feat_ref, own_ref, far_ref, sides_ref, far_sides_ref, bias_ref, far_bias_ref,
    out_ref, hid_ref, gw_ref, agg, w, cot, bias, grad_own,
):
    half = EDGE
    rows = own_ref.shape[0]

    def place(here, there):
        agg[:, here] = own_ref[...]
        agg[:, there] = far_ref[...]
        cot[:, here] = sides_ref[0:rows, :]
        cot[:, there] = far_sides_ref[0:rows, :]
        w[:, here] = sides_ref[rows:, :]
        w[:, there] = far_sides_ref[rows:, :]
        bias[:, here] = bias_ref[...]
        bias[:, there] = far_bias_ref[...]

    left, right = slice(0, half), slice(half, 2 * half)

    @pl.when(feat_ref[0] == 0)
    def _():
        place(left, right)

    @pl.when(feat_ref[0] == 1)
    def _():
        place(right, left)

    lane = pl.multiple_of(feat_ref[0] * half, half)
    pre = jnp.dot(agg[...], w[...], preferred_element_type=F32) + bias[0:1, :]
    sig = jax.nn.sigmoid(pre)
    value = (pre * sig).astype(BF16)
    slope = sig * (1.0 + pre * (1.0 - sig))
    grad = (cot[...].astype(F32) * slope).astype(BF16)

    @pl.when(feat_ref[0] == 0)
    def _():
        out_ref[...] = value[:, left]
        grad_own[...] = grad[:, left]

    @pl.when(feat_ref[0] == 1)
    def _():
        out_ref[...] = value[:, right]
        grad_own[...] = grad[:, right]

    w_rows = w[pl.ds(lane, half), :]
    hid_ref[...] = lax.dot_general(
        grad, w_rows, (((1,), (1,)), ((), ())), preferred_element_type=F32
    ).astype(BF16)
    own = grad_own[...]
    gw_ref[0:256, :] = scale * lax.dot_general(
        agg[...], own, (((0,), (0,)), ((), ())), preferred_element_type=F32
    )
    eighths = jnp.sum(own.astype(F32).reshape(-1, 8, half), axis=0)
    gw_ref[256:264, :] = jnp.broadcast_to(
        scale * jnp.sum(eighths, axis=0, keepdims=True), (8, half)
    )


def middle(scale, feat, own, far, sides, far_sides, bias, far_bias):
    rows = own.shape[0]
    vmem = pl.BlockSpec(memory_space=pltpu.VMEM)
    return pl.pallas_call(
        functools.partial(middle_kernel, scale),
        out_shape=[
            jax.ShapeDtypeStruct((rows, EDGE), BF16),
            jax.ShapeDtypeStruct((rows, EDGE), BF16),
            jax.ShapeDtypeStruct((264, EDGE), F32),
        ],
        in_specs=[pl.BlockSpec(memory_space=pltpu.SMEM)] + [vmem] * 6,
        out_specs=[vmem] * 3,
        scratch_shapes=[
            pltpu.VMEM((rows, 256), BF16),
            pltpu.VMEM((256, 256), BF16),
            pltpu.VMEM((rows, 256), BF16),
            pltpu.VMEM((8, 256), F32),
            pltpu.VMEM((rows, EDGE), BF16),
        ],
        compiler_params=pltpu.CompilerParams(vmem_limit_bytes=VMEM_LIMIT),
        name="middle",
    )(feat, own, far, sides, far_sides, bias, far_bias)


def on_device(tile_vals, tile_rows, tile_cols, tile_count, features, weight, bias_term, cotangent):
    tiles = tile_vals[0, 0]
    rows = tile_rows[0, 0]
    cols = tile_cols[0, 0]
    local_rows = features.shape[0]
    my_zhi, my_x = lax.axis_index("zhi"), lax.axis_index("x")
    my_y, my_zlo = lax.axis_index("y"), lax.axis_index("zlo")
    feat = lax.axis_index("feat").reshape(1)
    node_total = local_rows * 128
    scale = 1.0 / math.sqrt(node_total)

    with jax.named_scope("gather_row"):
        z2, z1, z3 = [pull(features, "zhi", 4, k) for k in (2, 1, 3)]
    with jax.named_scope("sides"):
        sides = jnp.concatenate([cotangent, weight], axis=0)
        bias = jnp.broadcast_to(bias_term[None, :], (8, EDGE))
        far_sides = pull(sides, "feat", 2, 1)
        far_bias = pull(bias, "feat", 2, 1)
    z1, z2, z3, far_sides, far_bias = lax.optimization_barrier(
        (z1, z2, z3, far_sides, far_bias)
    )
    with jax.named_scope("gather_row"):
        near = jnp.concatenate([features, z1], axis=0)
        away = jnp.concatenate([z3, z2], axis=0)
        near_blocks = [near] + [pull(near, "x", 4, k) for k in (1, 2, 3)]
        away_blocks = [away] + [pull(away, "x", 4, k) for k in (1, 2, 3)]
    near_blocks[0], rows, cols = lax.optimization_barrier((near, rows, cols))

    per = local_rows // EDGE
    row_block, col_block = rows // per, cols // per
    rel_y, rel_zlo = (row_block // 2 - my_y) % 4, (row_block % 2 - my_zlo) % 2
    row_at = (rel_y * 2 + rel_zlo) * per + rows % per
    rel_zhi, rel_x = (col_block // 4 - my_zhi) % 4, (col_block % 4 - my_x) % 4
    second = rel_zhi >= 2
    inner = jnp.where(second, 3 - rel_zhi, rel_zhi)
    col_at = (rel_x * 2 + inner) * per + cols % per
    packed, totals = slot_lists(row_at, col_at, second, tile_count[0, 0])
    lists = [packed[0], packed[1]]
    counts = [totals[0:1], totals[1:2]]

    wide = [jax.ShapeDtypeStruct((HALF_TILES, EDGE, EDGE), F32)]
    block = [jax.ShapeDtypeStruct((local_rows, EDGE), BF16)] * 8
    pair = [jax.ShapeDtypeStruct((2 * local_rows, EDGE), BF16)] * 4
    (base,) = tile_pass(
        tiles, lists[0], counts[0], near_blocks, None, wide, False, "forward_near"
    )
    partial_sums = tile_pass(
        tiles, lists[1], counts[1], away_blocks, base, block, False, "forward_away"
    )

    with jax.named_scope("scatter_col"):
        mine = [partial_sums[0]]
        for k in range(1, 8):
            mine.append(push_col(partial_sums[k], k // 2, k % 2))
    own = sum_blocks(mine, BF16, "sum_col")
    far = pull(own, "feat", 2, 1)
    outputs, hidden, grads = middle(scale, feat, own, far, sides, far_sides, bias, far_bias)

    with jax.named_scope("gather_col"):
        beside = pull(hidden, "zlo", 2, 1)
        blocks = [hidden, beside]
        along = [pull(hidden, "y", 4, k) for k in (1, 2, 3)]
        others = [pull(beside, "y", 4, k) for k in (1, 2, 3)]
        for k in range(3):
            blocks += [along[k], others[k]]
    with jax.named_scope("weight_grads"):
        grads = grads + pull(grads, "zlo", 2, 1)
        grads = lax.psum(grads, "x")
    back_away = tile_pass(
        tiles, lists[1], counts[1], blocks, None, pair, True, "backward_away"
    )
    back_away, grads = lax.optimization_barrier((back_away, grads))
    with jax.named_scope("weight_grads"):
        grads = lax.psum(grads, "y")
    with jax.named_scope("scatter_row_away"):
        got = [back_away[0]] + [push(back_away[k], "x", 4, k) for k in (1, 3, 2)]
    near_count, got[1] = lax.optimization_barrier((counts[0], got[1]))
    back_near = tile_pass(tiles, lists[0], near_count, blocks, None, pair, True, "backward_near")
    *got, back_near = lax.optimization_barrier((*got, back_near))
    z3, z2 = sum_pair(got, (BF16, BF16), "sum_away")
    z2, z3, back_near, grads = lax.optimization_barrier((z2, z3, back_near, grads))
    with jax.named_scope("weight_grads"):
        grads = lax.psum(grads, "zhi")
    with jax.named_scope("scatter_row_near"):
        near_got = [back_near[0]] + [push(back_near[k], "x", 4, k) for k in (1, 3, 2)]
    with jax.named_scope("scatter_row_away"):
        z2, z3 = push(z2, "zhi", 4, 2), push(z3, "zhi", 4, 3)
    z0, z1 = sum_pair(near_got, (F32, BF16), "sum_near")
    with jax.named_scope("scatter_row_near"):
        z1 = push(z1, "zhi", 4, 1)

    grad_feat = sum_blocks([z0, z1, z2, z3], BF16, "sum_z")
    return outputs, grad_feat, grads[:256], grads[256]


def solution(mesh):
    fine = Mesh(mesh.devices.reshape(4, 4, 4, 2, 2), ("zhi", "x", "y", "zlo", "feat"))
    row, col = ("zhi", "x"), ("y", "zlo")
    nodes = P(row + col, "feat")
    return jax.shard_map(
        on_device,
        mesh=fine,
        in_specs=(
            P(row, col, None, None, None),
            P(row, col, None),
            P(row, col, None),
            P(row, col),
            nodes,
            P(None, "feat"),
            P("feat"),
            nodes,
        ),
        out_specs=(nodes, nodes, P(None, "feat"), P("feat")),
        check_vma=False,
    )
```

profile of v0, /device:TPU:0, one launch (start us, length us, event | category | flops | bytes accessed | tf_op | source)
XLA Modules:
  0.0 262.9 jit_solution(10269760172767871733)
XLA Ops:
  7.2 5.5 %collective-permute-start.1 = (bf16[512,128]{1,0:T(8,128)(2,1)}, bf16[512,128]{1,0:T(8,128)(2,1)S(1)}, u32[]{:S(2)}, u32[]{:S(2)}) collective-permute-start(bf16[512,128]{1,0:T(8,128)(2,1)} %param.12), channel_id=1, source_target_pairs={{128,0},{192,64},{0,128},{64,192},{129,1},{193,65},{1,129},{65,193... | collective-permute-start | bytes 393224 | tf_op jit(solution)/shard_map/gather_row/ppermute | solution.py:22
  12.8 2.9 %collective-permute-start.2 = (bf16[512,128]{1,0:T(8,128)(2,1)}, bf16[512,128]{1,0:T(8,128)(2,1)S(1)}, u32[]{:S(2)}, u32[]{:S(2)}) collective-permute-start(bf16[512,128]{1,0:T(8,128)(2,1)} %param.12), channel_id=1, source_target_pairs={{192,0},{0,64},{64,128},{128,192},{193,1},{1,65},{65,129},{129,193... | collective-permute-start | bytes 393224 | tf_op jit(solution)/shard_map/gather_row/ppermute | solution.py:22
  21.8 3.7 %collective-permute-done = bf16[512,128]{1,0:T(8,128)(2,1)S(1)} collective-permute-done((bf16[512,128]{1,0:T(8,128)(2,1)}, bf16[512,128]{1,0:T(8,128)(2,1)S(1)}, u32[]{:S(2)}, u32[]{:S(2)}) %collective-permute-start) | collective-permute-done | bytes 131104 | tf_op jit(solution)/shard_map/gather_row/ppermute | solution.py:22
  27.1 2.7 %collective-permute-start.9 = (bf16[1024,128]{1,0:T(8,128)(2,1)S(1)}, bf16[1024,128]{1,0:T(8,128)(2,1)S(1)}, u32[]{:S(2)}, u32[]{:S(2)}) collective-permute-start(bf16[1024,128]{1,0:T(8,128)(2,1)S(1)} %constant_dynamic-update-slice_fusion.2.refs_0_), channel_id=1, source_target_pairs={{32,0},{48,16},{0,32},{16,48},{33,1},{49,17},{1,33},{17,49},{34,2}... | collective-permute-start | bytes 786440 | tf_op jit(solution)/shard_map/gather_row/ppermute | solution.py:22
  33.6 2.6 %collective-permute-done.10.refs_3_ = bf16[1024,128]{1,0:T(8,128)(2,1)S(1)} collective-permute-done((bf16[1024,128]{1,0:T(8,128)(2,1)S(1)}, bf16[1024,128]{1,0:T(8,128)(2,1)S(1)}, u32[]{:S(2)}, u32[]{:S(2)}) %collective-permute-start.10) | collective-permute-done | bytes 262176 | tf_op jit(solution)/shard_map/gather_row/ppermute | solution.py:22
  38.1 4.5 %collective-permute-done.9.refs_2_ = bf16[1024,128]{1,0:T(8,128)(2,1)S(1)} collective-permute-done((bf16[1024,128]{1,0:T(8,128)(2,1)S(1)}, bf16[1024,128]{1,0:T(8,128)(2,1)S(1)}, u32[]{:S(2)}, u32[]{:S(2)}) %collective-permute-start.9) | collective-permute-done | bytes 262176 | tf_op jit(solution)/shard_map/gather_row/ppermute | solution.py:22
  42.7 3.7 %forward_near.1.refs_4_ = f32[32,128,128]{2,1,0:T(8,128)S(1)} custom-call(s32[1]{0:T(128)} %get-tuple-element.85.total_ref, s32[384]{0:T(512)S(1)} %get-tuple-element.110.list_ref, bf16[384,128,128]{2,1,0:T(8,128)(2,1)} %bitcast.6, bf16[1024,128]{1,0:T(8,128)(2,1)S(1)} %constant_dynamic-update-slice_fusion.2.refs_0_, ...), custom_call_target="tpu_custom_call" | custom-call | flops 1610612736 | bytes 12582912 | tf_op jit(solution)/shard_map/forward_near/pallas_call | solution.py:114
  46.4 6.5 %collective-permute-done.6.refs_2_ = bf16[1024,128]{1,0:T(8,128)(2,1)S(1)} collective-permute-done((bf16[1024,128]{1,0:T(8,128)(2,1)S(1)}, bf16[1024,128]{1,0:T(8,128)(2,1)S(1)}, u32[]{:S(2)}, u32[]{:S(2)}) %collective-permute-start.6) | collective-permute-done | bytes 262176 | tf_op jit(solution)/shard_map/gather_row/ppermute | solution.py:22
  52.9 3.6 %forward_away.1 = (bf16[512,128]{1,0:T(8,128)(2,1)S(1)}, bf16[512,128]{1,0:T(8,128)(2,1)S(1)}, bf16[512,128]{1,0:T(8,128)(2,1)S(1)}, bf16[512,128]{1,0:T(8,128)(...) custom-call(s32[1]{0:T(128)} %get-tuple-element.117.total_ref, ...), custom_call_target="tpu_custom_call" | custom-call | flops 1610612736 | bytes 12582912 | tf_op jit(solution)/shard_map/forward_away/pallas_call | solution.py:114
  58.8 3.9 %collective-permute-start.13 = (bf16[512,128]{1,0:T(8,128)(2,1)S(1)}, bf16[512,128]{1,0:T(8,128)(2,1)S(1)}, u32[]{:S(2)}, u32[]{:S(2)}) collective-permute-start(bf16[512,128]{1,0:T(8,128)(2,1)S(1)} %get-tuple-element.66), channel_id=1, source_target_pairs={{0,6},{2,4},{4,10},{6,8},{8,14},{10,12},{12,2},{14,0},{1,7},{3,5},... | collective-permute-start | bytes 393224 | tf_op jit(solution)/shard_map/scatter_col/ppermute | solution.py:34
  63.0 2.8 %collective-permute-start.15 = (bf16[512,128]{1,0:T(8,128)(2,1)S(1)}, bf16[512,128]{1,0:T(8,128)(2,1)S(1)}, u32[]{:S(2)}, u32[]{:S(2)}) collective-permute-start(bf16[512,128]{1,0:T(8,128)(2,1)S(1)} %get-tuple-element.68), channel_id=1, source_target_pairs={{0,10},{2,8},{4,14},{6,12},{8,2},{10,0},{12,6},{14,4},{1,11},{3,9}... | collective-permute-start | bytes 393224 | tf_op jit(solution)/shard_map/scatter_col/ppermute | solution.py:34
  68.9 3.1 %collective-permute-start.17 = (bf16[512,128]{1,0:T(8,128)(2,1)S(1)}, bf16[512,128]{1,0:T(8,128)(2,1)S(1)}, u32[]{:S(2)}, u32[]{:S(2)}) collective-permute-start(bf16[512,128]{1,0:T(8,128)(2,1)S(1)} %get-tuple-element.70), channel_id=1, source_target_pairs={{0,14},{2,12},{4,2},{6,0},{8,6},{10,4},{12,10},{14,8},{1,15},{3,13... | collective-permute-start | bytes 393224 | tf_op jit(solution)/shard_map/scatter_col/ppermute | solution.py:34
  80.6 2.5 collective-permute-start.24
  85.0 2.6 collective-permute-start.20
  89.5 3.4 %collective-permute-start.23 = (bf16[512,128]{1,0:T(8,128)(2,1)S(1)}, bf16[512,128]{1,0:T(8,128)(2,1)S(1)}, u32[]{:S(2)}, u32[]{:S(2)}) collective-permute-start(bf16[512,128]{1,0:T(8,128)(2,1)S(1)} %collective-permute-done.19.refs_1_), channel_id=1, source_target_pairs={{8,0},{12,4},{0,8},{4,12},{9,1},{13,5},{1,9},{5,13},{10,2},{14,6},... | collective-permute-start | bytes 393224 | tf_op jit(solution)/shard_map/gather_col/ppermute | solution.py:22
  97.8 4.1 %backward_away.1 = (bf16[1024,128]{1,0:T(8,128)(2,1)S(1)}, bf16[1024,128]{1,0:T(8,128)(2,1)S(1)}, bf16[1024,128]{1,0:T(8,128)(2,1)S(1)}, bf16[1024,128]{1,0:T(8,128)(2,1)}) custom-call(s32[1]{0:T(128)} %get-tuple-element.117.total_ref, s32[384]{0:T(512)S(1)} %get-tuple-element.111.list_ref, bf16[384,128,128]{2,1,0:T(8,128)(2,1)} %bitcast.8, ...), custom_call_target="tpu_custom_call" | custom-call | flops 1610612736 | bytes 12582912 | tf_op jit(solution)/shard_map/backward_away/pallas_call | solution.py:114
  102.0 37.9 %all-reduce.4.cloned.1.call-done = f32[264,128]{1,0:T(8,128)} async-done(((f32[264,128]{1,0:T(8,128)}), f32[264,128]{1,0:T(8,128)}) %all-reduce.4.cloned.1.call-update) | async-done | bytes 135184 | tf_op jit(solution)/shard_map/weight_grads/psum | solution.py:325
  143.8 6.1 %collective-permute-done.27.refs_1_ = bf16[1024,128]{1,0:T(8,128)(2,1)S(1)} collective-permute-done((bf16[1024,128]{1,0:T(8,128)(2,1)S(1)}, bf16[1024,128]{1,0:T(8,128)(2,1)S(1)}, u32[]{:S(2)}, u32[]{:S(2)}) %collective-permute-start.27) | collective-permute-done | bytes 262176 | tf_op jit(solution)/shard_map/scatter_row_away/ppermute | solution.py:26
  150.0 3.7 %backward_near.1 = (bf16[1024,128]{1,0:T(8,128)(2,1)S(1)}, bf16[1024,128]{1,0:T(8,128)(2,1)S(1)}, bf16[1024,128]{1,0:T(8,128)(2,1)S(1)}, bf16[1024,128]{1,0:T(8,128)(2,1)S(1)}) custom-call(s32[1]{0:T(128)} %get-tuple-element.85.total_ref, s32[384]{0:T(512)S(1)} %get-tuple-element.110.list_ref, bf16[384,128,128]{2,1,0:T(8,128)(2,1)} %bitcast.9, ...), custom_call_target="tpu_custom_call" | custom-call | flops 1610612736 | bytes 12582912 | tf_op jit(solution)/shard_map/backward_near/pallas_call | solution.py:114
  153.8 36.9 %all-reduce.6.cloned.1.call-done = f32[264,128]{1,0:T(8,128)} async-done(((f32[264,128]{1,0:T(8,128)}), f32[264,128]{1,0:T(8,128)}) %all-reduce.6.cloned.1.call-update) | async-done | bytes 135184 | tf_op jit(solution)/shard_map/weight_grads/psum | solution.py:331
  195.7 5.8 %collective-permute-start.34 = (bf16[512,128]{1,0:T(8,128)(2,1)S(1)}, bf16[512,128]{1,0:T(8,128)(2,1)S(1)}, u32[]{:S(2)}, u32[]{:S(2)}) collective-permute-start(bf16[512,128]{1,0:T(8,128)(2,1)S(1)} %get-tuple-element.107), channel_id=1, source_target_pairs={{0,128},{64,192},{128,0},{192,64},{1,129},{65,193},{129,1},{193,65... | collective-permute-start | bytes 393224 | tf_op jit(solution)/shard_map/scatter_row_away/ppermute | solution.py:26
  201.9 43.0 %all-reduce.8.cloned.1.call-done = f32[264,128]{1,0:T(8,128)} async-done(((f32[264,128]{1,0:T(8,128)}), f32[264,128]{1,0:T(8,128)}) %all-reduce.8.cloned.1.call-update) | async-done | bytes 135184 | tf_op jit(solution)/shard_map/weight_grads/psum | solution.py:340
  246.6 3.1 %collective-permute-start.33 = (bf16[512,128]{1,0:T(8,128)(2,1)S(1)}, bf16[512,128]{1,0:T(8,128)(2,1)S(1)}, u32[]{:S(2)}, u32[]{:S(2)}) collective-permute-start(bf16[512,128]{1,0:T(8,128)(2,1)S(1)} %get-tuple-element.106), channel_id=1, source_target_pairs={{0,64},{64,128},{128,192},{192,0},{1,65},{65,129},{129,193},{193,1... | collective-permute-start | bytes 393224 | tf_op jit(solution)/shard_map/scatter_row_near/ppermute | solution.py:26
  251.0 4.7 %collective-permute-done.33.refs_1_ = bf16[512,128]{1,0:T(8,128)(2,1)S(1)} collective-permute-done((bf16[512,128]{1,0:T(8,128)(2,1)S(1)}, bf16[512,128]{1,0:T(8,128)(2,1)S(1)}, u32[]{:S(2)}, u32[]{:S(2)}) %collective-permute-start.33) | collective-permute-done | bytes 131104 | tf_op jit(solution)/shard_map/scatter_row_near/ppermute | solution.py:26
  (90 shorter events, 48.9 us)
Async XLA Ops:
  7.2 132.7 %all-reduce.4.cloned.1.call-start = ((), (), s32[]{:S(2)}) async-start(), calls=%async_computation | async-start | bytes 270336 | tf_op jit(solution)/shard_map/weight_grads/psum | solution.py:325
  7.2 14.5 %collective-permute-start.1 = (bf16[512,128]{1,0:T(8,128)(2,1)}, bf16[512,128]{1,0:T(8,128)(2,1)S(1)}, u32[]{:S(2)}, u32[]{:S(2)}) collective-permute-start(bf16[512,128]{1,0:T(8,128)(2,1)} %param.12), channel_id=1, source_target_pairs={{128,0},{192,64},{0,128},{64,192},{129,1},{193,65},{1,129},{65,193... | collective-permute-start | bytes 393224 | tf_op jit(solution)/shard_map/gather_row/ppermute | solution.py:22
  12.8 12.7 %collective-permute-start = (bf16[512,128]{1,0:T(8,128)(2,1)}, bf16[512,128]{1,0:T(8,128)(2,1)S(1)}, u32[]{:S(2)}, u32[]{:S(2)}) collective-permute-start(bf16[512,128]{1,0:T(8,128)(2,1)} %param.12), channel_id=1, source_target_pairs={{64,0},{128,64},{192,128},{0,192},{65,1},{129,65},{193,129},{1,193... | collective-permute-start | bytes 393224 | tf_op jit(solution)/shard_map/gather_row/ppermute | solution.py:22
  12.8 12.7 %collective-permute-start.2 = (bf16[512,128]{1,0:T(8,128)(2,1)}, bf16[512,128]{1,0:T(8,128)(2,1)S(1)}, u32[]{:S(2)}, u32[]{:S(2)}) collective-permute-start(bf16[512,128]{1,0:T(8,128)(2,1)} %param.12), channel_id=1, source_target_pairs={{192,0},{0,64},{64,128},{128,192},{193,1},{1,65},{65,129},{129,193... | collective-permute-start | bytes 393224 | tf_op jit(solution)/shard_map/gather_row/ppermute | solution.py:22
  25.5 10.7 %collective-permute-start.10 = (bf16[1024,128]{1,0:T(8,128)(2,1)S(1)}, bf16[1024,128]{1,0:T(8,128)(2,1)S(1)}, u32[]{:S(2)}, u32[]{:S(2)}) collective-permute-start(bf16[1024,128]{1,0:T(8,128)(2,1)S(1)} %constant_dynamic-update-slice_fusion.2.refs_0_), channel_id=1, source_target_pairs={{48,0},{0,16},{16,32},{32,48},{49,1},{1,17},{17,33},{33,49},{50,2}... | collective-permute-start | bytes 786440 | tf_op jit(solution)/shard_map/gather_row/ppermute | solution.py:22
  27.1 15.5 %collective-permute-start.9 = (bf16[1024,128]{1,0:T(8,128)(2,1)S(1)}, bf16[1024,128]{1,0:T(8,128)(2,1)S(1)}, u32[]{:S(2)}, u32[]{:S(2)}) collective-permute-start(bf16[1024,128]{1,0:T(8,128)(2,1)S(1)} %constant_dynamic-update-slice_fusion.2.refs_0_), channel_id=1, source_target_pairs={{32,0},{48,16},{0,32},{16,48},{33,1},{49,17},{1,33},{17,49},{34,2}... | collective-permute-start | bytes 786440 | tf_op jit(solution)/shard_map/gather_row/ppermute | solution.py:22
  29.8 12.8 %collective-permute-start.8 = (bf16[1024,128]{1,0:T(8,128)(2,1)S(1)}, bf16[1024,128]{1,0:T(8,128)(2,1)S(1)}, u32[]{:S(2)}, u32[]{:S(2)}) collective-permute-start(bf16[1024,128]{1,0:T(8,128)(2,1)S(1)} %constant_dynamic-update-slice_fusion.2.refs_0_), channel_id=1, source_target_pairs={{16,0},{32,16},{48,32},{0,48},{17,1},{33,17},{49,33},{1,49},{18,2}... | collective-permute-start | bytes 786440 | tf_op jit(solution)/shard_map/gather_row/ppermute | solution.py:22
  31.3 15.0 %collective-permute-start.7 = (bf16[1024,128]{1,0:T(8,128)(2,1)S(1)}, bf16[1024,128]{1,0:T(8,128)(2,1)S(1)}, u32[]{:S(2)}, u32[]{:S(2)}) collective-permute-start(bf16[1024,128]{1,0:T(8,128)(2,1)S(1)} %constant_dynamic-update-slice_fusion.4.refs_0_), channel_id=1, source_target_pairs={{48,0},{0,16},{16,32},{32,48},{49,1},{1,17},{17,33},{33,49},{50,2}... | collective-permute-start | bytes 786440 | tf_op jit(solution)/shard_map/gather_row/ppermute | solution.py:22
  32.0 20.9 %collective-permute-start.6 = (bf16[1024,128]{1,0:T(8,128)(2,1)S(1)}, bf16[1024,128]{1,0:T(8,128)(2,1)S(1)}, u32[]{:S(2)}, u32[]{:S(2)}) collective-permute-start(bf16[1024,128]{1,0:T(8,128)(2,1)S(1)} %constant_dynamic-update-slice_fusion.4.refs_0_), channel_id=1, source_target_pairs={{32,0},{48,16},{0,32},{16,48},{33,1},{49,17},{1,33},{17,49},{34,2}... | collective-permute-start | bytes 786440 | tf_op jit(solution)/shard_map/gather_row/ppermute | solution.py:22
  36.2 16.6 %collective-permute-start.5 = (bf16[1024,128]{1,0:T(8,128)(2,1)S(1)}, bf16[1024,128]{1,0:T(8,128)(2,1)S(1)}, u32[]{:S(2)}, u32[]{:S(2)}) collective-permute-start(bf16[1024,128]{1,0:T(8,128)(2,1)S(1)} %constant_dynamic-update-slice_fusion.4.refs_0_), channel_id=1, source_target_pairs={{16,0},{32,16},{48,32},{0,48},{17,1},{33,17},{49,33},{1,49},{18,2}... | collective-permute-start | bytes 786440 | tf_op jit(solution)/shard_map/gather_row/ppermute | solution.py:22
  58.6 10.3 %collective-permute-start.12 = (bf16[512,128]{1,0:T(8,128)(2,1)S(1)}, bf16[512,128]{1,0:T(8,128)(2,1)S(1)}, u32[]{:S(2)}, u32[]{:S(2)}) collective-permute-start(bf16[512,128]{1,0:T(8,128)(2,1)S(1)} %get-tuple-element.65), channel_id=1, source_target_pairs={{0,4},{2,6},{4,8},{6,10},{8,12},{10,14},{12,0},{14,2},{1,5},{3,7},... | collective-permute-start | bytes 393224 | tf_op jit(solution)/shard_map/scatter_col/ppermute | solution.py:34
  58.8 13.1 %collective-permute-start.13 = (bf16[512,128]{1,0:T(8,128)(2,1)S(1)}, bf16[512,128]{1,0:T(8,128)(2,1)S(1)}, u32[]{:S(2)}, u32[]{:S(2)}) collective-permute-start(bf16[512,128]{1,0:T(8,128)(2,1)S(1)} %get-tuple-element.66), channel_id=1, source_target_pairs={{0,6},{2,4},{4,10},{6,8},{8,14},{10,12},{12,2},{14,0},{1,7},{3,5},... | collective-permute-start | bytes 393224 | tf_op jit(solution)/shard_map/scatter_col/ppermute | solution.py:34
  62.7 10.3 %collective-permute-start.14 = (bf16[512,128]{1,0:T(8,128)(2,1)S(1)}, bf16[512,128]{1,0:T(8,128)(2,1)S(1)}, u32[]{:S(2)}, u32[]{:S(2)}) collective-permute-start(bf16[512,128]{1,0:T(8,128)(2,1)S(1)} %get-tuple-element.67), channel_id=1, source_target_pairs={{0,8},{2,10},{4,12},{6,14},{8,0},{10,2},{12,4},{14,6},{1,9},{3,11}... | collective-permute-start | bytes 393224 | tf_op jit(solution)/shard_map/scatter_col/ppermute | solution.py:34
  78.5 14.3 %collective-permute-start.26 = (f32[264,128]{1,0:T(8,128)S(1)}, f32[264,128]{1,0:T(8,128)S(1)}, u32[]{:S(2)}, u32[]{:S(2)}) collective-permute-start(f32[264,128]{1,0:T(8,128)S(1)} %get-tuple-element.79), channel_id=1, source_target_pairs={{2,0},{0,2},{3,1},{1,3},{6,4},{4,6},{7,5},{5,7},{10,8},{8,10},{11,... | collective-permute-start | bytes 405512 | tf_op jit(solution)/shard_map/weight_grads/ppermute | solution.py:22
  83.0 11.8 %collective-permute-start.22 = (bf16[512,128]{1,0:T(8,128)(2,1)S(1)}, bf16[512,128]{1,0:T(8,128)(2,1)S(1)}, u32[]{:S(2)}, u32[]{:S(2)}) collective-permute-start(bf16[512,128]{1,0:T(8,128)(2,1)S(1)} %get-tuple-element.74.refs_0_), channel_id=1, source_target_pairs={{8,0},{12,4},{0,8},{4,12},{9,1},{13,5},{1,9},{5,13},{10,2},{14,6},... | collective-permute-start | bytes 393224 | tf_op jit(solution)/shard_map/gather_col/ppermute | solution.py:22
  94.8 95.9 %all-reduce.6.cloned.1.call-start = ((), (), s32[]{:S(2)}) async-start(), calls=%async_computation.1 | async-start | bytes 270336 | tf_op jit(solution)/shard_map/weight_grads/psum | solution.py:331
  141.1 12.6 %collective-permute-start.28 = (bf16[1024,128]{1,0:T(8,128)(2,1)}, bf16[1024,128]{1,0:T(8,128)(2,1)S(1)}, u32[]{:S(2)}, u32[]{:S(2)}) collective-permute-start(bf16[1024,128]{1,0:T(8,128)(2,1)} %get-tuple-element.83), channel_id=1, source_target_pairs={{0,48},{16,0},{32,16},{48,32},{1,49},{17,1},{33,17},{49,33},{2,50}... | collective-permute-start | bytes 786440 | tf_op jit(solution)/shard_map/scatter_row_away/ppermute | solution.py:26
  143.1 10.6 %collective-permute-start.29 = (bf16[1024,128]{1,0:T(8,128)(2,1)S(1)}, bf16[1024,128]{1,0:T(8,128)(2,1)S(1)}, u32[]{:S(2)}, u32[]{:S(2)}) collective-permute-start(bf16[1024,128]{1,0:T(8,128)(2,1)S(1)} %get-tuple-element.84), channel_id=1, source_target_pairs={{0,32},{16,48},{32,0},{48,16},{1,33},{17,49},{33,1},{49,17},{2,34}... | collective-permute-start | bytes 786440 | tf_op jit(solution)/shard_map/scatter_row_away/ppermute | solution.py:26
  143.8 101.1 %all-reduce.8.cloned.1.call-start = ((), (), s32[]{:S(2)}) async-start(), calls=%async_computation.2 | async-start | bytes 270336 | tf_op jit(solution)/shard_map/weight_grads/psum | solution.py:340
  190.7 55.8 %collective-permute-start.30 = (bf16[1024,128]{1,0:T(8,128)(2,1)S(1)}, bf16[1024,128]{1,0:T(8,128)(2,1)S(1)}, u32[]{:S(2)}, u32[]{:S(2)}) collective-permute-start(bf16[1024,128]{1,0:T(8,128)(2,1)S(1)} %get-tuple-element.102), channel_id=1, source_target_pairs={{0,16},{16,32},{32,48},{48,0},{1,17},{17,33},{33,49},{49,1},{2,18}... | collective-permute-start | bytes 786440 | tf_op jit(solution)/shard_map/scatter_row_near/ppermute | solution.py:26
  192.2 54.3 %collective-permute-start.31 = (bf16[1024,128]{1,0:T(8,128)(2,1)S(1)}, bf16[1024,128]{1,0:T(8,128)(2,1)S(1)}, u32[]{:S(2)}, u32[]{:S(2)}) collective-permute-start(bf16[1024,128]{1,0:T(8,128)(2,1)S(1)} %get-tuple-element.103), channel_id=1, source_target_pairs={{0,48},{16,0},{32,16},{48,32},{1,49},{17,1},{33,17},{49,33},{2,50}... | collective-permute-start | bytes 786440 | tf_op jit(solution)/shard_map/scatter_row_near/ppermute | solution.py:26
  193.9 52.5 %collective-permute-start.32 = (bf16[1024,128]{1,0:T(8,128)(2,1)S(1)}, bf16[1024,128]{1,0:T(8,128)(2,1)S(1)}, u32[]{:S(2)}, u32[]{:S(2)}) collective-permute-start(bf16[1024,128]{1,0:T(8,128)(2,1)S(1)} %get-tuple-element.104), channel_id=1, source_target_pairs={{0,32},{16,48},{32,0},{48,16},{1,33},{17,49},{33,1},{49,17},{2,34}... | collective-permute-start | bytes 786440 | tf_op jit(solution)/shard_map/scatter_row_near/ppermute | solution.py:26
  195.7 55.2 %collective-permute-start.34 = (bf16[512,128]{1,0:T(8,128)(2,1)S(1)}, bf16[512,128]{1,0:T(8,128)(2,1)S(1)}, u32[]{:S(2)}, u32[]{:S(2)}) collective-permute-start(bf16[512,128]{1,0:T(8,128)(2,1)S(1)} %get-tuple-element.107), channel_id=1, source_target_pairs={{0,128},{64,192},{128,0},{192,64},{1,129},{65,193},{129,1},{193,65... | collective-permute-start | bytes 393224 | tf_op jit(solution)/shard_map/scatter_row_away/ppermute | solution.py:26
  201.5 49.4 %collective-permute-start.35 = (bf16[512,128]{1,0:T(8,128)(2,1)S(1)}, bf16[512,128]{1,0:T(8,128)(2,1)S(1)}, u32[]{:S(2)}, u32[]{:S(2)}) collective-permute-start(bf16[512,128]{1,0:T(8,128)(2,1)S(1)} %get-tuple-element.108), channel_id=1, source_target_pairs={{0,192},{64,0},{128,64},{192,128},{1,193},{65,1},{129,65},{193,129... | collective-permute-start | bytes 393224 | tf_op jit(solution)/shard_map/scatter_row_away/ppermute | solution.py:26
  (15 other events, 115.3 us)
Sparse Core Ops, SparseCore 0:
  94.9 44.8 all-reduce.3
  143.9 46.7 all-reduce.5
  195.8 49.0 all-reduce.7
where the time goes:
time: 266 us; the launch traced here: 263 us
  waiting for transfers between devices  157 us (59%)
  starting transfers between devices  64.8 us (24%)
  Pallas kernels  17.3 us (7%)
  between operations  14.6 us (5%)
  local copies, waits for them, and re-layouts  6.76 us (3%)
  other arithmetic  2.89 us (1%)
    psum x1, waiting for transfers between devices, on_device(): grads = lax.psum(grads, 'zhi')  43 us
    psum x1, waiting for transfers between devices, on_device(): grads = lax.psum(grads, 'x')  37.9 us
    psum x1, waiting for transfers between devices, on_device(): grads = lax.psum(grads, 'y')  36.9 us
    ppermute x20, starting transfers between devices, pull(): lax.ppermute(value, axis, [((i + step) % size, i) for i in range(size)])  33.3 us
    ppermute x20, waiting for transfers between devices, pull(): lax.ppermute(value, axis, [((i + step) % size, i) for i in range(size)])  21.7 us
    ppermute x9, starting transfers between devices, push(): lax.ppermute(value, axis, [(i, (i + step) % size) for i in range(size)])  18.3 us
    pallas_call x4, Pallas kernels, tile_pass(): pl.pallas_call(functools.partial(tile_kernel, transpose, len(sources), le...  15.1 us
    ppermute x7, starting transfers between devices, push_col(): return lax.ppermute(value, ('y', 'zlo'), pairs)  13.1 us
  transfers between devices with their start and end apart: 39, of which 16 were waited for; matrix products, arithmetic and copies ran while one was open for 4% of the time, Pallas kernels for 4%

commit v1 on v0

--- a/solution.py
+++ b/solution.py
@@ -32,6 +32,11 @@
         for z in range(2):
             pairs.append((y * 2 + z, ((y + step_y) % 4) * 2 + (z + step_z) % 2))
     return lax.ppermute(value, ("y", "zlo"), pairs)
+
+
+def pair_sum(value, axis, size, flip):
+    with jax.named_scope("weight_grads"):
+        return value + lax.ppermute(value, axis, [(i, i ^ flip) for i in range(size)])
 
 
 def slot_lists(rows, cols, second, live):
@@ -320,31 +325,34 @@
         others = [pull(beside, "y", 4, k) for k in (1, 2, 3)]
         for k in range(3):
             blocks += [along[k], others[k]]
-    with jax.named_scope("weight_grads"):
-        grads = grads + pull(grads, "zlo", 2, 1)
-        grads = lax.psum(grads, "x")
+    grads = pair_sum(grads, "zlo", 2, 1)
+    blocks[1], grads = lax.optimization_barrier((blocks[1], grads))
+    grads = pair_sum(grads, "x", 4, 1)
+    grads = pair_sum(grads, "x", 4, 2)
     back_away = tile_pass(
         tiles, lists[1], counts[1], blocks, None, pair, True, "backward_away"
     )
     back_away, grads = lax.optimization_barrier((back_away, grads))
-    with jax.named_scope("weight_grads"):
-        grads = lax.psum(grads, "y")
     with jax.named_scope("scatter_row_away"):
         got = [back_away[0]] + [push(back_away[k], "x", 4, k) for k in (1, 3, 2)]
+    grads = pair_sum(grads, "zhi", 4, 1)
     near_count, got[1] = lax.optimization_barrier((counts[0], got[1]))
     back_near = tile_pass(tiles, lists[0], near_count, blocks, None, pair, True, "backward_near")
-    *got, back_near = lax.optimization_barrier((*got, back_near))
+    *got, back_near, grads = lax.optimization_barrier((*got, back_near, grads))
+    grads = pair_sum(grads, "zhi", 4, 2)
     z3, z2 = sum_pair(got, (BF16, BF16), "sum_away")
-    z2, z3, back_near, grads = lax.optimization_barrier((z2, z3, back_near, grads))
-    with jax.named_scope("weight_grads"):
-        grads = lax.psum(grads, "zhi")
+    z2, z3, back_near = lax.optimization_barrier((z2, z3, back_near))
     with jax.named_scope("scatter_row_near"):
         near_got = [back_near[0]] + [push(back_near[k], "x", 4, k) for k in (1, 3, 2)]
     with jax.named_scope("scatter_row_away"):
         z2, z3 = push(z2, "zhi", 4, 2), push(z3, "zhi", 4, 3)
+    near_got[1], grads = lax.optimization_barrier((near_got[1], grads))
+    grads = pair_sum(grads, "y", 4, 1)
+    *near_got, z2, z3 = lax.optimization_barrier((*near_got, z2, z3))
     z0, z1 = sum_pair(near_got, (F32, BF16), "sum_near")
     with jax.named_scope("scatter_row_near"):
         z1 = push(z1, "zhi", 4, 1)
+    grads = pair_sum(grads, "y", 4, 2)
 
     grad_feat = sum_blocks([z0, z1, z2, z3], BF16, "sum_z")
     return outputs, grad_feat, grads[:256], grads[256]

time: 266 us -> 164 us (0.62)
  waiting for transfers between devices: 157 us -> 52.5 us
  starting transfers between devices: 64.8 us -> 83.1 us
  between operations: 14.6 us -> 1.5 us
    psum x3 -> x0, waiting for transfers between devices: 118 us -> none  [the longest x1 43 us: on_device(): grads = lax.psum(grads, 'zhi')]
    ppermute x0 -> x7, starting transfers between devices: none -> 14.4 us  [pair_sum(): lax.ppermute(value, axis, [(i, i ^ flip) for i in range(size)])]
    ppermute x9, waiting for transfers between devices: 10.9 us -> 18.7 us  [push(): lax.ppermute(value, axis, [(i, (i + step) % size) for i in range(size)])]
    ppermute x0 -> x7, waiting for transfers between devices: none -> 5.87 us  [pair_sum(): lax.ppermute(value, axis, [(i, i ^ flip) for i in range(size)])]
    ppermute x9, starting transfers between devices: 18.3 us -> 23.2 us  [push(): lax.ppermute(value, axis, [(i, (i + step) % size) for i in range(size)])]
    ppermute x20 -> x19, starting transfers between devices: 33.3 us -> 28.6 us  [pull(): lax.ppermute(value, axis, [((i + step) % size, i) for i in range(size)])]
    ppermute x20 -> x19, waiting for transfers between devices: 21.7 us -> 25.5 us  [pull(): lax.ppermute(value, axis, [((i + step) % size, i) for i in range(size)])]
    ppermute x7, waiting for transfers between devices: 6.27 us -> 2.52 us  [push_col(): return lax.ppermute(value, ('y', 'zlo'), pairs)]
  transfers between devices with their start and end apart: 39 -> 42, of which waited for: 16 -> 19; matrix products, arithmetic and copies ran while one was open for 4% -> 4% of each run, Pallas kernels for 4% -> 7%
where the time goes in v1:
time: 164 us; the launch traced here: 161 us
  starting transfers between devices  83.1 us (51%)
  waiting for transfers between devices  52.5 us (32%)
  Pallas kernels  16.2 us (10%)
  local copies, waits for them, and re-layouts  5.18 us (3%)
  other arithmetic  2.34 us (1%)
    ppermute x19, starting transfers between devices, pull(): lax.ppermute(value, axis, [((i + step) % size, i) for i in range(size)])  28.6 us
    ppermute x19, waiting for transfers between devices, pull(): lax.ppermute(value, axis, [((i + step) % size, i) for i in range(size)])  25.5 us
    ppermute x9, starting transfers between devices, push(): lax.ppermute(value, axis, [(i, (i + step) % size) for i in range(size)])  23.2 us
    ppermute x9, waiting for transfers between devices, push(): lax.ppermute(value, axis, [(i, (i + step) % size) for i in range(size)])  18.7 us
    ppermute x7, starting transfers between devices, push_col(): return lax.ppermute(value, ('y', 'zlo'), pairs)  16.8 us
    ppermute x7, starting transfers between devices, pair_sum(): lax.ppermute(value, axis, [(i, i ^ flip) for i in range(size)])  14.4 us
    pallas_call x4, Pallas kernels, tile_pass(): pl.pallas_call(functools.partial(tile_kernel, transpose, len(sources), le...  14 us
    ppermute x7, waiting for transfers between devices, pair_sum(): lax.ppermute(value, axis, [(i, i ^ flip) for i in range(size)])  5.87 us
  transfers between devices with their start and end apart: 42, of which 19 were waited for; matrix products, arithmetic and copies ran while one was open for 4% of the time, Pallas kernels for 7%

profile of v1, /device:TPU:0, one launch (start us, length us, event | category | flops | bytes accessed | tf_op | source)
XLA Modules:
  0.0 160.8 jit_solution(15809377035133946433)
XLA Ops:
  0.6 5.5 %collective-permute-start.1 = (bf16[512,128]{1,0:T(8,128)(2,1)}, bf16[512,128]{1,0:T(8,128)(2,1)S(1)}, u32[]{:S(2)}, u32[]{:S(2)}) collective-permute-start(bf16[512,128]{1,0:T(8,128)(2,1)} %param.12), channel_id=1, source_target_pairs={{128,0},{192,64},{0,128},{64,192},{129,1},{193,65},{1,129},{65,193... | collective-permute-start | bytes 393224 | tf_op jit(solution)/shard_map/gather_row/ppermute | solution.py:22
  6.2 2.9 %collective-permute-start.2 = (bf16[512,128]{1,0:T(8,128)(2,1)}, bf16[512,128]{1,0:T(8,128)(2,1)S(1)}, u32[]{:S(2)}, u32[]{:S(2)}) collective-permute-start(bf16[512,128]{1,0:T(8,128)(2,1)} %param.12), channel_id=1, source_target_pairs={{192,0},{0,64},{64,128},{128,192},{193,1},{1,65},{65,129},{129,193... | collective-permute-start | bytes 393224 | tf_op jit(solution)/shard_map/gather_row/ppermute | solution.py:22
  15.2 3.7 %collective-permute-done = bf16[512,128]{1,0:T(8,128)(2,1)S(1)} collective-permute-done((bf16[512,128]{1,0:T(8,128)(2,1)}, bf16[512,128]{1,0:T(8,128)(2,1)S(1)}, u32[]{:S(2)}, u32[]{:S(2)}) %collective-permute-start) | collective-permute-done | bytes 131104 | tf_op jit(solution)/shard_map/gather_row/ppermute | solution.py:22
  20.5 2.7 %collective-permute-start.9 = (bf16[1024,128]{1,0:T(8,128)(2,1)S(1)}, bf16[1024,128]{1,0:T(8,128)(2,1)S(1)}, u32[]{:S(2)}, u32[]{:S(2)}) collective-permute-start(bf16[1024,128]{1,0:T(8,128)(2,1)S(1)} %constant_dynamic-update-slice_fusion.2.refs_0_), channel_id=1, source_target_pairs={{32,0},{48,16},{0,32},{16,48},{33,1},{49,17},{1,33},{17,49},{34,2}... | collective-permute-start | bytes 786440 | tf_op jit(solution)/shard_map/gather_row/ppermute | solution.py:22
  31.6 4.5 %collective-permute-done.9.refs_2_ = bf16[1024,128]{1,0:T(8,128)(2,1)S(1)} collective-permute-done((bf16[1024,128]{1,0:T(8,128)(2,1)S(1)}, bf16[1024,128]{1,0:T(8,128)(2,1)S(1)}, u32[]{:S(2)}, u32[]{:S(2)}) %collective-permute-start.9) | collective-permute-done | bytes 262176 | tf_op jit(solution)/shard_map/gather_row/ppermute | solution.py:22
  36.1 3.0 %forward_near.1.refs_4_ = f32[32,128,128]{2,1,0:T(8,128)S(1)} custom-call(s32[1]{0:T(128)} %get-tuple-element.97.total_ref, s32[384]{0:T(512)S(1)} %get-tuple-element.130.list_ref, bf16[384,128,128]{2,1,0:T(8,128)(2,1)} %bitcast.6, bf16[1024,128]{1,0:T(8,128)(2,1)S(1)} %constant_dynamic-update-slice_fusion.2.refs_0_, ...), custom_call_target="tpu_custom_call" | custom-call | flops 1610612736 | bytes 12582912 | tf_op jit(solution)/shard_map/forward_near/pallas_call | solution.py:119
  39.7 6.6 %collective-permute-done.6.refs_2_ = bf16[1024,128]{1,0:T(8,128)(2,1)S(1)} collective-permute-done((bf16[1024,128]{1,0:T(8,128)(2,1)S(1)}, bf16[1024,128]{1,0:T(8,128)(2,1)S(1)}, u32[]{:S(2)}, u32[]{:S(2)}) %collective-permute-start.6) | collective-permute-done | bytes 262176 | tf_op jit(solution)/shard_map/gather_row/ppermute | solution.py:22
  46.3 4.1 %forward_away.1 = (bf16[512,128]{1,0:T(8,128)(2,1)S(1)}, bf16[512,128]{1,0:T(8,128)(2,1)S(1)}, bf16[512,128]{1,0:T(8,128)(2,1)S(1)}, bf16[512,128]{1,0:T(8,128)(...) custom-call(s32[1]{0:T(128)} %get-tuple-element.137.total_ref, ...), custom_call_target="tpu_custom_call" | custom-call | flops 1610612736 | bytes 12582912 | tf_op jit(solution)/shard_map/forward_away/pallas_call | solution.py:119
  55.0 2.8 %collective-permute-start.14 = (bf16[512,128]{1,0:T(8,128)(2,1)S(1)}, bf16[512,128]{1,0:T(8,128)(2,1)S(1)}, u32[]{:S(2)}, u32[]{:S(2)}) collective-permute-start(bf16[512,128]{1,0:T(8,128)(2,1)S(1)} %get-tuple-element.77), channel_id=1, source_target_pairs={{0,8},{2,10},{4,12},{6,14},{8,0},{10,2},{12,4},{14,6},{1,9},{3,11}... | collective-permute-start | bytes 393224 | tf_op jit(solution)/shard_map/scatter_col/ppermute | solution.py:34
  58.0 2.8 %collective-permute-start.16 = (bf16[512,128]{1,0:T(8,128)(2,1)S(1)}, bf16[512,128]{1,0:T(8,128)(2,1)S(1)}, u32[]{:S(2)}, u32[]{:S(2)}) collective-permute-start(bf16[512,128]{1,0:T(8,128)(2,1)S(1)} %get-tuple-element.79), channel_id=1, source_target_pairs={{0,12},{2,14},{4,0},{6,2},{8,4},{10,6},{12,8},{14,10},{1,13},{3,15... | collective-permute-start | bytes 393224 | tf_op jit(solution)/shard_map/scatter_col/ppermute | solution.py:34
  60.8 6.5 %collective-permute-start.17 = (bf16[512,128]{1,0:T(8,128)(2,1)S(1)}, bf16[512,128]{1,0:T(8,128)(2,1)S(1)}, u32[]{:S(2)}, u32[]{:S(2)}) collective-permute-start(bf16[512,128]{1,0:T(8,128)(2,1)S(1)} %get-tuple-element.80), channel_id=1, source_target_pairs={{0,14},{2,12},{4,2},{6,0},{8,6},{10,4},{12,10},{14,8},{1,15},{3,13... | collective-permute-start | bytes 393224 | tf_op jit(solution)/shard_map/scatter_col/ppermute | solution.py:34
  74.5 4.4 %collective-permute-done.20 = f32[264,128]{1,0:T(8,128)S(1)} collective-permute-done((f32[264,128]{1,0:T(8,128)S(1)}, f32[264,128]{1,0:T(8,128)S(1)}, u32[]{:S(2)}, u32[]{:S(2)}) %collective-permute-start.20) | collective-permute-done | bytes 135200 | tf_op jit(solution)/shard_map/weight_grads/ppermute | solution.py:39
  80.9 3.3 %collective-permute-start.27 = (f32[264,128]{1,0:T(8,128)S(1)}, f32[264,128]{1,0:T(8,128)S(1)}, u32[]{:S(2)}, u32[]{:S(2)}) collective-permute-start(f32[264,128]{1,0:T(8,128)S(1)} %add.91), channel_id=1, source_target_pairs={{0,16},{16,0},{32,48},{48,32},{1,17},{17,1},{33,49},{49,33},{2,18}... | collective-permute-start | bytes 405512 | tf_op jit(solution)/shard_map/weight_grads/ppermute | solution.py:39
  85.8 3.8 %collective-permute-start.23 = (bf16[512,128]{1,0:T(8,128)(2,1)S(1)}, bf16[512,128]{1,0:T(8,128)(2,1)S(1)}, u32[]{:S(2)}, u32[]{:S(2)}) collective-permute-start(bf16[512,128]{1,0:T(8,128)(2,1)S(1)} %get-tuple-element.84.refs_0_), channel_id=1, source_target_pairs={{8,0},{12,4},{0,8},{4,12},{9,1},{13,5},{1,9},{5,13},{10,2},{14,6},... | collective-permute-start | bytes 393224 | tf_op jit(solution)/shard_map/gather_col/ppermute | solution.py:22
  100.5 3.9 %backward_away.1 = (bf16[1024,128]{1,0:T(8,128)(2,1)S(1)}, bf16[1024,128]{1,0:T(8,128)(2,1)S(1)}, bf16[1024,128]{1,0:T(8,128)(2,1)S(1)}, bf16[1024,128]{1,0:T(8,128)(2,1)S(1)}) custom-call(s32[1]{0:T(128)} %get-tuple-element.137.total_ref, s32[384]{0:T(512)S(1)} %get-tuple-element.131.list_ref, bf16[384,128,128]{2,1,0:T(8,128)(2,1)} %bitcast.8, ...), custom_call_target="tpu_custom_call" | custom-call | flops 1610612736 | bytes 12582912 | tf_op jit(solution)/shard_map/backward_away/pallas_call | solution.py:119
  104.7 3.3 %collective-permute-start.32 = (f32[264,128]{1,0:T(8,128)S(1)}, f32[264,128]{1,0:T(8,128)S(1)}, u32[]{:S(2)}, u32[]{:S(2)}) collective-permute-start(f32[264,128]{1,0:T(8,128)S(1)} %add.93), channel_id=1, source_target_pairs={{0,64},{64,0},{128,192},{192,128},{1,65},{65,1},{129,193},{193,129... | collective-permute-start | bytes 405512 | tf_op jit(solution)/shard_map/weight_grads/ppermute | solution.py:39
  108.0 4.1 %collective-permute-start.30 = (bf16[1024,128]{1,0:T(8,128)(2,1)S(1)}, bf16[1024,128]{1,0:T(8,128)(2,1)S(1)}, u32[]{:S(2)}, u32[]{:S(2)}) collective-permute-start(bf16[1024,128]{1,0:T(8,128)(2,1)S(1)} %get-tuple-element.95), channel_id=1, source_target_pairs={{0,48},{16,0},{32,16},{48,32},{1,49},{17,1},{33,17},{49,33},{2,50}... | collective-permute-start | bytes 786440 | tf_op jit(solution)/shard_map/scatter_row_away/ppermute | solution.py:26
  113.4 5.6 %collective-permute-done.29.refs_1_ = bf16[1024,128]{1,0:T(8,128)(2,1)S(1)} collective-permute-done((bf16[1024,128]{1,0:T(8,128)(2,1)S(1)}, bf16[1024,128]{1,0:T(8,128)(2,1)S(1)}, u32[]{:S(2)}, u32[]{:S(2)}) %collective-permute-start.29) | collective-permute-done | bytes 262176 | tf_op jit(solution)/shard_map/scatter_row_away/ppermute | solution.py:26
  119.0 3.0 %backward_near.1 = (bf16[1024,128]{1,0:T(8,128)(2,1)S(1)}, bf16[1024,128]{1,0:T(8,128)(2,1)S(1)}, bf16[1024,128]{1,0:T(8,128)(2,1)S(1)}, bf16[1024,128]{1,0:T(8,128)(2,1)S(1)}) custom-call(s32[1]{0:T(128)} %get-tuple-element.97.total_ref, s32[384]{0:T(512)S(1)} %get-tuple-element.130.list_ref, bf16[384,128,128]{2,1,0:T(8,128)(2,1)} %bitcast.9, ...), custom_call_target="tpu_custom_call" | custom-call | flops 1610612736 | bytes 12582912 | tf_op jit(solution)/shard_map/backward_near/pallas_call | solution.py:119
  128.2 2.7 %collective-permute-start.36 = (bf16[1024,128]{1,0:T(8,128)(2,1)S(1)}, bf16[1024,128]{1,0:T(8,128)(2,1)S(1)}, u32[]{:S(2)}, u32[]{:S(2)}) collective-permute-start(bf16[1024,128]{1,0:T(8,128)(2,1)S(1)} %get-tuple-element.118), channel_id=1, source_target_pairs={{0,32},{16,48},{32,0},{48,16},{1,33},{17,49},{33,1},{49,17},{2,34}... | collective-permute-start | bytes 786440 | tf_op jit(solution)/shard_map/scatter_row_near/ppermute | solution.py:26
  132.9 3.8 %collective-permute-start.37 = (bf16[512,128]{1,0:T(8,128)(2,1)S(1)}, bf16[512,128]{1,0:T(8,128)(2,1)S(1)}, u32[]{:S(2)}, u32[]{:S(2)}) collective-permute-start(bf16[512,128]{1,0:T(8,128)(2,1)S(1)} %get-tuple-element.119), channel_id=1, source_target_pairs={{0,128},{64,192},{128,0},{192,64},{1,129},{65,193},{129,1},{193,65... | collective-permute-start | bytes 393224 | tf_op jit(solution)/shard_map/scatter_row_away/ppermute | solution.py:26
  136.7 5.7 %collective-permute-start.38 = (bf16[512,128]{1,0:T(8,128)(2,1)S(1)}, bf16[512,128]{1,0:T(8,128)(2,1)S(1)}, u32[]{:S(2)}, u32[]{:S(2)}) collective-permute-start(bf16[512,128]{1,0:T(8,128)(2,1)S(1)} %get-tuple-element.120), channel_id=1, source_target_pairs={{0,192},{64,0},{128,64},{192,128},{1,193},{65,1},{129,65},{193,129... | collective-permute-start | bytes 393224 | tf_op jit(solution)/shard_map/scatter_row_away/ppermute | solution.py:26
  144.5 5.7 %collective-permute-done.38.refs_3_ = bf16[512,128]{1,0:T(8,128)(2,1)S(1)} collective-permute-done((bf16[512,128]{1,0:T(8,128)(2,1)S(1)}, bf16[512,128]{1,0:T(8,128)(2,1)S(1)}, u32[]{:S(2)}, u32[]{:S(2)}) %collective-permute-start.38) | collective-permute-done | bytes 131104 | tf_op jit(solution)/shard_map/scatter_row_away/ppermute | solution.py:26
  152.1 6.8 %collective-permute-done.39.refs_1_ = bf16[512,128]{1,0:T(8,128)(2,1)S(1)} collective-permute-done((bf16[512,128]{1,0:T(8,128)(2,1)S(1)}, bf16[512,128]{1,0:T(8,128)(2,1)S(1)}, u32[]{:S(2)}, u32[]{:S(2)}) %collective-permute-start.39) | collective-permute-done | bytes 131104 | tf_op jit(solution)/shard_map/scatter_row_near/ppermute | solution.py:26
  (99 shorter events, 58.1 us)
Async XLA Ops:
  0.6 14.5 %collective-permute-start.1 = (bf16[512,128]{1,0:T(8,128)(2,1)}, bf16[512,128]{1,0:T(8,128)(2,1)S(1)}, u32[]{:S(2)}, u32[]{:S(2)}) collective-permute-start(bf16[512,128]{1,0:T(8,128)(2,1)} %param.12), channel_id=1, source_target_pairs={{128,0},{192,64},{0,128},{64,192},{129,1},{193,65},{1,129},{65,193... | collective-permute-start | bytes 393224 | tf_op jit(solution)/shard_map/gather_row/ppermute | solution.py:22
  6.2 12.7 %collective-permute-start = (bf16[512,128]{1,0:T(8,128)(2,1)}, bf16[512,128]{1,0:T(8,128)(2,1)S(1)}, u32[]{:S(2)}, u32[]{:S(2)}) collective-permute-start(bf16[512,128]{1,0:T(8,128)(2,1)} %param.12), channel_id=1, source_target_pairs={{64,0},{128,64},{192,128},{0,192},{65,1},{129,65},{193,129},{1,193... | collective-permute-start | bytes 393224 | tf_op jit(solution)/shard_map/gather_row/ppermute | solution.py:22
  6.2 12.7 %collective-permute-start.2 = (bf16[512,128]{1,0:T(8,128)(2,1)}, bf16[512,128]{1,0:T(8,128)(2,1)S(1)}, u32[]{:S(2)}, u32[]{:S(2)}) collective-permute-start(bf16[512,128]{1,0:T(8,128)(2,1)} %param.12), channel_id=1, source_target_pairs={{192,0},{0,64},{64,128},{128,192},{193,1},{1,65},{65,129},{129,193... | collective-permute-start | bytes 393224 | tf_op jit(solution)/shard_map/gather_row/ppermute | solution.py:22
  19.0 10.7 %collective-permute-start.10 = (bf16[1024,128]{1,0:T(8,128)(2,1)S(1)}, bf16[1024,128]{1,0:T(8,128)(2,1)S(1)}, u32[]{:S(2)}, u32[]{:S(2)}) collective-permute-start(bf16[1024,128]{1,0:T(8,128)(2,1)S(1)} %constant_dynamic-update-slice_fusion.2.refs_0_), channel_id=1, source_target_pairs={{48,0},{0,16},{16,32},{32,48},{49,1},{1,17},{17,33},{33,49},{50,2}... | collective-permute-start | bytes 786440 | tf_op jit(solution)/shard_map/gather_row/ppermute | solution.py:22
  20.5 15.5 %collective-permute-start.9 = (bf16[1024,128]{1,0:T(8,128)(2,1)S(1)}, bf16[1024,128]{1,0:T(8,128)(2,1)S(1)}, u32[]{:S(2)}, u32[]{:S(2)}) collective-permute-start(bf16[1024,128]{1,0:T(8,128)(2,1)S(1)} %constant_dynamic-update-slice_fusion.2.refs_0_), channel_id=1, source_target_pairs={{32,0},{48,16},{0,32},{16,48},{33,1},{49,17},{1,33},{17,49},{34,2}... | collective-permute-start | bytes 786440 | tf_op jit(solution)/shard_map/gather_row/ppermute | solution.py:22
  23.3 12.8 %collective-permute-start.8 = (bf16[1024,128]{1,0:T(8,128)(2,1)S(1)}, bf16[1024,128]{1,0:T(8,128)(2,1)S(1)}, u32[]{:S(2)}, u32[]{:S(2)}) collective-permute-start(bf16[1024,128]{1,0:T(8,128)(2,1)S(1)} %constant_dynamic-update-slice_fusion.2.refs_0_), channel_id=1, source_target_pairs={{16,0},{32,16},{48,32},{0,48},{17,1},{33,17},{49,33},{1,49},{18,2}... | collective-permute-start | bytes 786440 | tf_op jit(solution)/shard_map/gather_row/ppermute | solution.py:22
  24.7 14.9 %collective-permute-start.7 = (bf16[1024,128]{1,0:T(8,128)(2,1)S(1)}, bf16[1024,128]{1,0:T(8,128)(2,1)S(1)}, u32[]{:S(2)}, u32[]{:S(2)}) collective-permute-start(bf16[1024,128]{1,0:T(8,128)(2,1)S(1)} %constant_dynamic-update-slice_fusion.4.refs_0_), channel_id=1, source_target_pairs={{48,0},{0,16},{16,32},{32,48},{49,1},{1,17},{17,33},{33,49},{50,2}... | collective-permute-start | bytes 786440 | tf_op jit(solution)/shard_map/gather_row/ppermute | solution.py:22
  25.4 20.9 %collective-permute-start.6 = (bf16[1024,128]{1,0:T(8,128)(2,1)S(1)}, bf16[1024,128]{1,0:T(8,128)(2,1)S(1)}, u32[]{:S(2)}, u32[]{:S(2)}) collective-permute-start(bf16[1024,128]{1,0:T(8,128)(2,1)S(1)} %constant_dynamic-update-slice_fusion.4.refs_0_), channel_id=1, source_target_pairs={{32,0},{48,16},{0,32},{16,48},{33,1},{49,17},{1,33},{17,49},{34,2}... | collective-permute-start | bytes 786440 | tf_op jit(solution)/shard_map/gather_row/ppermute | solution.py:22
  29.7 16.6 %collective-permute-start.5 = (bf16[1024,128]{1,0:T(8,128)(2,1)S(1)}, bf16[1024,128]{1,0:T(8,128)(2,1)S(1)}, u32[]{:S(2)}, u32[]{:S(2)}) collective-permute-start(bf16[1024,128]{1,0:T(8,128)(2,1)S(1)} %constant_dynamic-update-slice_fusion.4.refs_0_), channel_id=1, source_target_pairs={{16,0},{32,16},{48,32},{0,48},{17,1},{33,17},{49,33},{1,49},{18,2}... | collective-permute-start | bytes 786440 | tf_op jit(solution)/shard_map/gather_row/ppermute | solution.py:22
  50.8 9.9 %collective-permute-start.12 = (bf16[512,128]{1,0:T(8,128)(2,1)S(1)}, bf16[512,128]{1,0:T(8,128)(2,1)S(1)}, u32[]{:S(2)}, u32[]{:S(2)}) collective-permute-start(bf16[512,128]{1,0:T(8,128)(2,1)S(1)} %get-tuple-element.75), channel_id=1, source_target_pairs={{0,4},{2,6},{4,8},{6,10},{8,12},{10,14},{12,0},{14,2},{1,5},{3,7},... | collective-permute-start | bytes 393224 | tf_op jit(solution)/shard_map/scatter_col/ppermute | solution.py:34
  52.4 14.8 %collective-permute-start.13 = (bf16[512,128]{1,0:T(8,128)(2,1)S(1)}, bf16[512,128]{1,0:T(8,128)(2,1)S(1)}, u32[]{:S(2)}, u32[]{:S(2)}) collective-permute-start(bf16[512,128]{1,0:T(8,128)(2,1)S(1)} %get-tuple-element.76), channel_id=1, source_target_pairs={{0,6},{2,4},{4,10},{6,8},{8,14},{10,12},{12,2},{14,0},{1,7},{3,5},... | collective-permute-start | bytes 393224 | tf_op jit(solution)/shard_map/scatter_col/ppermute | solution.py:34
  55.0 12.6 %collective-permute-start.14 = (bf16[512,128]{1,0:T(8,128)(2,1)S(1)}, bf16[512,128]{1,0:T(8,128)(2,1)S(1)}, u32[]{:S(2)}, u32[]{:S(2)}) collective-permute-start(bf16[512,128]{1,0:T(8,128)(2,1)S(1)} %get-tuple-element.77), channel_id=1, source_target_pairs={{0,8},{2,10},{4,12},{6,14},{8,0},{10,2},{12,4},{14,6},{1,9},{3,11}... | collective-permute-start | bytes 393224 | tf_op jit(solution)/shard_map/scatter_col/ppermute | solution.py:34
  58.0 11.3 %collective-permute-start.16 = (bf16[512,128]{1,0:T(8,128)(2,1)S(1)}, bf16[512,128]{1,0:T(8,128)(2,1)S(1)}, u32[]{:S(2)}, u32[]{:S(2)}) collective-permute-start(bf16[512,128]{1,0:T(8,128)(2,1)S(1)} %get-tuple-element.79), channel_id=1, source_target_pairs={{0,12},{2,14},{4,0},{6,2},{8,4},{10,6},{12,8},{14,10},{1,13},{3,15... | collective-permute-start | bytes 393224 | tf_op jit(solution)/shard_map/scatter_col/ppermute | solution.py:34
  80.9 12.6 %collective-permute-start.27 = (f32[264,128]{1,0:T(8,128)S(1)}, f32[264,128]{1,0:T(8,128)S(1)}, u32[]{:S(2)}, u32[]{:S(2)}) collective-permute-start(f32[264,128]{1,0:T(8,128)S(1)} %add.91), channel_id=1, source_target_pairs={{0,16},{16,0},{32,48},{48,32},{1,17},{17,1},{33,49},{49,33},{2,18}... | collective-permute-start | bytes 405512 | tf_op jit(solution)/shard_map/weight_grads/ppermute | solution.py:39
  85.8 11.1 %collective-permute-start.23 = (bf16[512,128]{1,0:T(8,128)(2,1)S(1)}, bf16[512,128]{1,0:T(8,128)(2,1)S(1)}, u32[]{:S(2)}, u32[]{:S(2)}) collective-permute-start(bf16[512,128]{1,0:T(8,128)(2,1)S(1)} %get-tuple-element.84.refs_0_), channel_id=1, source_target_pairs={{8,0},{12,4},{0,8},{4,12},{9,1},{13,5},{1,9},{5,13},{10,2},{14,6},... | collective-permute-start | bytes 393224 | tf_op jit(solution)/shard_map/gather_col/ppermute | solution.py:22
  104.4 14.6 %collective-permute-start.29 = (bf16[1024,128]{1,0:T(8,128)(2,1)S(1)}, bf16[1024,128]{1,0:T(8,128)(2,1)S(1)}, u32[]{:S(2)}, u32[]{:S(2)}) collective-permute-start(bf16[1024,128]{1,0:T(8,128)(2,1)S(1)} %get-tuple-element.93), channel_id=1, source_target_pairs={{0,16},{16,32},{32,48},{48,0},{1,17},{17,33},{33,49},{49,1},{2,18}... | collective-permute-start | bytes 786440 | tf_op jit(solution)/shard_map/scatter_row_away/ppermute | solution.py:26
  108.0 14.0 %collective-permute-start.30 = (bf16[1024,128]{1,0:T(8,128)(2,1)S(1)}, bf16[1024,128]{1,0:T(8,128)(2,1)S(1)}, u32[]{:S(2)}, u32[]{:S(2)}) collective-permute-start(bf16[1024,128]{1,0:T(8,128)(2,1)S(1)} %get-tuple-element.95), channel_id=1, source_target_pairs={{0,48},{16,0},{32,16},{48,32},{1,49},{17,1},{33,17},{49,33},{2,50}... | collective-permute-start | bytes 786440 | tf_op jit(solution)/shard_map/scatter_row_away/ppermute | solution.py:26
  112.1 10.0 %collective-permute-start.31 = (bf16[1024,128]{1,0:T(8,128)(2,1)S(1)}, bf16[1024,128]{1,0:T(8,128)(2,1)S(1)}, u32[]{:S(2)}, u32[]{:S(2)}) collective-permute-start(bf16[1024,128]{1,0:T(8,128)(2,1)S(1)} %get-tuple-element.96), channel_id=1, source_target_pairs={{0,32},{16,48},{32,0},{48,16},{1,33},{17,49},{33,1},{49,17},{2,34}... | collective-permute-start | bytes 786440 | tf_op jit(solution)/shard_map/scatter_row_away/ppermute | solution.py:26
  122.2 10.7 %collective-permute-start.33 = (bf16[1024,128]{1,0:T(8,128)(2,1)S(1)}, bf16[1024,128]{1,0:T(8,128)(2,1)S(1)}, u32[]{:S(2)}, u32[]{:S(2)}) collective-permute-start(bf16[1024,128]{1,0:T(8,128)(2,1)S(1)} %get-tuple-element.114), channel_id=1, source_target_pairs={{0,16},{16,32},{32,48},{48,0},{1,17},{17,33},{33,49},{49,1},{2,18}... | collective-permute-start | bytes 786440 | tf_op jit(solution)/shard_map/scatter_row_near/ppermute | solution.py:26
  125.7 24.5 %collective-permute-start.35 = (bf16[1024,128]{1,0:T(8,128)(2,1)S(1)}, bf16[1024,128]{1,0:T(8,128)(2,1)S(1)}, u32[]{:S(2)}, u32[]{:S(2)}) collective-permute-start(bf16[1024,128]{1,0:T(8,128)(2,1)S(1)} %get-tuple-element.117), channel_id=1, source_target_pairs={{0,48},{16,0},{32,16},{48,32},{1,49},{17,1},{33,17},{49,33},{2,50}... | collective-permute-start | bytes 786440 | tf_op jit(solution)/shard_map/scatter_row_near/ppermute | solution.py:26
  128.2 22.0 %collective-permute-start.36 = (bf16[1024,128]{1,0:T(8,128)(2,1)S(1)}, bf16[1024,128]{1,0:T(8,128)(2,1)S(1)}, u32[]{:S(2)}, u32[]{:S(2)}) collective-permute-start(bf16[1024,128]{1,0:T(8,128)(2,1)S(1)} %get-tuple-element.118), channel_id=1, source_target_pairs={{0,32},{16,48},{32,0},{48,16},{1,33},{17,49},{33,1},{49,17},{2,34}... | collective-permute-start | bytes 786440 | tf_op jit(solution)/shard_map/scatter_row_near/ppermute | solution.py:26
  132.9 11.6 %collective-permute-start.37 = (bf16[512,128]{1,0:T(8,128)(2,1)S(1)}, bf16[512,128]{1,0:T(8,128)(2,1)S(1)}, u32[]{:S(2)}, u32[]{:S(2)}) collective-permute-start(bf16[512,128]{1,0:T(8,128)(2,1)S(1)} %get-tuple-element.119), channel_id=1, source_target_pairs={{0,128},{64,192},{128,0},{192,64},{1,129},{65,193},{129,1},{193,65... | collective-permute-start | bytes 393224 | tf_op jit(solution)/shard_map/scatter_row_away/ppermute | solution.py:26
  136.7 13.5 %collective-permute-start.38 = (bf16[512,128]{1,0:T(8,128)(2,1)S(1)}, bf16[512,128]{1,0:T(8,128)(2,1)S(1)}, u32[]{:S(2)}, u32[]{:S(2)}) collective-permute-start(bf16[512,128]{1,0:T(8,128)(2,1)S(1)} %get-tuple-element.120), channel_id=1, source_target_pairs={{0,192},{64,0},{128,64},{192,128},{1,193},{65,1},{129,65},{193,129... | collective-permute-start | bytes 393224 | tf_op jit(solution)/shard_map/scatter_row_away/ppermute | solution.py:26
  142.5 17.1 %collective-permute-start.41 = (f32[264,128]{1,0:T(8,128)S(1)}, f32[264,128]{1,0:T(8,128)S(1)}, u32[]{:S(2)}, u32[]{:S(2)}) collective-permute-start(f32[264,128]{1,0:T(8,128)S(1)} %add.96), channel_id=1, source_target_pairs={{0,8},{4,12},{8,0},{12,4},{1,9},{5,13},{9,1},{13,5},{2,10},{6,14},... | collective-permute-start | bytes 405512 | tf_op jit(solution)/shard_map/weight_grads/ppermute | solution.py:39
  (18 other events, 140.2 us)

commit v2 on v1

--- a/solution.py
+++ b/solution.py
@@ -32,6 +32,12 @@
         for z in range(2):
             pairs.append((y * 2 + z, ((y + step_y) % 4) * 2 + (z + step_z) % 2))
     return lax.ppermute(value, ("y", "zlo"), pairs)
+
+
+def group_sum(value, axis, size):
+    with jax.named_scope("weight_grads"):
+        parts = [pull(value, axis, size, k) for k in (1, 2, 3)]
+        return (value + parts[1]) + (parts[0] + parts[2])
 
 
 def pair_sum(value, axis, size, flip):
@@ -326,9 +332,7 @@
         for k in range(3):
             blocks += [along[k], others[k]]
     grads = pair_sum(grads, "zlo", 2, 1)
-    blocks[1], grads = lax.optimization_barrier((blocks[1], grads))
-    grads = pair_sum(grads, "x", 4, 1)
-    grads = pair_sum(grads, "x", 4, 2)
+    grads = group_sum(grads, "x", 4)
     back_away = tile_pass(
         tiles, lists[1], counts[1], blocks, None, pair, True, "backward_away"
     )
@@ -347,12 +351,10 @@
     with jax.named_scope("scatter_row_away"):
         z2, z3 = push(z2, "zhi", 4, 2), push(z3, "zhi", 4, 3)
     near_got[1], grads = lax.optimization_barrier((near_got[1], grads))
-    grads = pair_sum(grads, "y", 4, 1)
-    *near_got, z2, z3 = lax.optimization_barrier((*near_got, z2, z3))
+    grads = group_sum(grads, "y", 4)
     z0, z1 = sum_pair(near_got, (F32, BF16), "sum_near")
     with jax.named_scope("scatter_row_near"):
         z1 = push(z1, "zhi", 4, 1)
-    grads = pair_sum(grads, "y", 4, 2)
 
     grad_feat = sum_blocks([z0, z1, z2, z3], BF16, "sum_z")
     return outputs, grad_feat, grads[:256], grads[256]

time: 164 us -> 153 us (0.933)
  the two profiles are of different devices: /device:TPU:0 before, /device:TPU:2 now
where the time goes in v2:
time: 153 us; the launch traced here: 151 us
  starting transfers between devices  80.9 us (53%)
  waiting for transfers between devices  43.6 us (28%)
  Pallas kernels  17.9 us (12%)
  local copies, waits for them, and re-layouts  5.18 us (3%)
  other arithmetic  2.32 us (2%)
  between operations  1.57 us (1%)
    ppermute x25, starting transfers between devices, pull(): lax.ppermute(value, axis, [((i + step) % size, i) for i in range(size)])  43.9 us
    ppermute x25, waiting for transfers between devices, pull(): lax.ppermute(value, axis, [((i + step) % size, i) for i in range(size)])  21 us
    ppermute x9, starting transfers between devices, push(): lax.ppermute(value, axis, [(i, (i + step) % size) for i in range(size)])  16.7 us
    pallas_call x4, Pallas kernels, tile_pass(): pl.pallas_call(functools.partial(tile_kernel, transpose, len(sources), le...  15.7 us
    ppermute x7, starting transfers between devices, push_col(): return lax.ppermute(value, ('y', 'zlo'), pairs)  14 us
    ppermute x9, waiting for transfers between devices, push(): lax.ppermute(value, axis, [(i, (i + step) % size) for i in range(size)])  13.5 us
    ppermute x3, starting transfers between devices, pair_sum(): lax.ppermute(value, axis, [(i, i ^ flip) for i in range(size)])  6.33 us
    ppermute x7, waiting for transfers between devices, push_col(): return lax.ppermute(value, ('y', 'zlo'), pairs)  5.31 us
  transfers between devices with their start and end apart: 44, of which 16 were waited for; matrix products, arithmetic and copies ran while one was open for 4% of the time, Pallas kernels for 8%

profile of v2, /device:TPU:2, one launch (start us, length us, event | category | flops | bytes accessed | tf_op | source)
XLA Modules:
  0.0 151.4 jit_solution(8475235672735409763)
XLA Ops:
  0.6 7.3 %collective-permute-start.1 = (bf16[512,128]{1,0:T(8,128)(2,1)}, bf16[512,128]{1,0:T(8,128)(2,1)S(1)}, u32[]{:S(2)}, u32[]{:S(2)}) collective-permute-start(bf16[512,128]{1,0:T(8,128)(2,1)} %param.12), channel_id=1, source_target_pairs={{128,0},{192,64},{0,128},{64,192},{129,1},{193,65},{1,129},{65,193... | collective-permute-start | bytes 393224 | tf_op jit(solution)/shard_map/gather_row/ppermute | solution.py:22
  7.9 2.9 %collective-permute-start.2 = (bf16[512,128]{1,0:T(8,128)(2,1)}, bf16[512,128]{1,0:T(8,128)(2,1)S(1)}, u32[]{:S(2)}, u32[]{:S(2)}) collective-permute-start(bf16[512,128]{1,0:T(8,128)(2,1)} %param.12), channel_id=1, source_target_pairs={{192,0},{0,64},{64,128},{128,192},{193,1},{1,65},{65,129},{129,193... | collective-permute-start | bytes 393224 | tf_op jit(solution)/shard_map/gather_row/ppermute | solution.py:22
  16.9 3.7 %collective-permute-done = bf16[512,128]{1,0:T(8,128)(2,1)S(1)} collective-permute-done((bf16[512,128]{1,0:T(8,128)(2,1)}, bf16[512,128]{1,0:T(8,128)(2,1)S(1)}, u32[]{:S(2)}, u32[]{:S(2)}) %collective-permute-start) | collective-permute-done | bytes 131104 | tf_op jit(solution)/shard_map/gather_row/ppermute | solution.py:22
  25.7 3.5 %collective-permute-start.6 = (bf16[1024,128]{1,0:T(8,128)(2,1)S(1)}, bf16[1024,128]{1,0:T(8,128)(2,1)S(1)}, u32[]{:S(2)}, u32[]{:S(2)}) collective-permute-start(bf16[1024,128]{1,0:T(8,128)(2,1)S(1)} %constant_dynamic-update-slice_fusion.4.refs_0_), channel_id=1, source_target_pairs={{32,0},{48,16},{0,32},{16,48},{33,1},{49,17},{1,33},{17,49},{34,2}... | collective-permute-start | bytes 786440 | tf_op jit(solution)/shard_map/gather_row/ppermute | solution.py:22
  29.9 4.2 %collective-permute-done.10.refs_3_ = bf16[1024,128]{1,0:T(8,128)(2,1)S(1)} collective-permute-done((bf16[1024,128]{1,0:T(8,128)(2,1)S(1)}, bf16[1024,128]{1,0:T(8,128)(2,1)S(1)}, u32[]{:S(2)}, u32[]{:S(2)}) %collective-permute-start.10) | collective-permute-done | bytes 262176 | tf_op jit(solution)/shard_map/gather_row/ppermute | solution.py:22
  34.7 7.2 %collective-permute-done.8.refs_1_ = bf16[1024,128]{1,0:T(8,128)(2,1)S(1)} collective-permute-done((bf16[1024,128]{1,0:T(8,128)(2,1)S(1)}, bf16[1024,128]{1,0:T(8,128)(2,1)S(1)}, u32[]{:S(2)}, u32[]{:S(2)}) %collective-permute-start.8) | collective-permute-done | bytes 262176 | tf_op jit(solution)/shard_map/gather_row/ppermute | solution.py:22
  41.8 3.9 %forward_near.1.refs_4_ = f32[32,128,128]{2,1,0:T(8,128)S(1)} custom-call(s32[1]{0:T(128)} %get-tuple-element.87.total_ref, s32[384]{0:T(512)S(1)} %get-tuple-element.114.list_ref, bf16[384,128,128]{2,1,0:T(8,128)(2,1)} %bitcast.6, bf16[1024,128]{1,0:T(8,128)(2,1)S(1)} %constant_dynamic-update-slice_fusion.2.refs_0_, ...), custom_call_target="tpu_custom_call" | custom-call | flops 1610612736 | bytes 12582912 | tf_op jit(solution)/shard_map/forward_near/pallas_call | solution.py:125
  47.8 4.1 %forward_away.1 = (bf16[512,128]{1,0:T(8,128)(2,1)S(1)}, bf16[512,128]{1,0:T(8,128)(2,1)S(1)}, bf16[512,128]{1,0:T(8,128)(2,1)S(1)}, bf16[512,128]{1,0:T(8,128)(...) custom-call(s32[1]{0:T(128)} %get-tuple-element.121.total_ref, ...), custom_call_target="tpu_custom_call" | custom-call | flops 1610612736 | bytes 12582912 | tf_op jit(solution)/shard_map/forward_away/pallas_call | solution.py:125
  52.0 3.0 %collective-permute-start.12 = (bf16[512,128]{1,0:T(8,128)(2,1)S(1)}, bf16[512,128]{1,0:T(8,128)(2,1)S(1)}, u32[]{:S(2)}, u32[]{:S(2)}) collective-permute-start(bf16[512,128]{1,0:T(8,128)(2,1)S(1)} %get-tuple-element.67), channel_id=1, source_target_pairs={{0,4},{2,6},{4,8},{6,10},{8,12},{10,14},{12,0},{14,2},{1,5},{3,7},... | collective-permute-start | bytes 393224 | tf_op jit(solution)/shard_map/scatter_col/ppermute | solution.py:34
  55.1 2.9 %collective-permute-start.13 = (bf16[512,128]{1,0:T(8,128)(2,1)S(1)}, bf16[512,128]{1,0:T(8,128)(2,1)S(1)}, u32[]{:S(2)}, u32[]{:S(2)}) collective-permute-start(bf16[512,128]{1,0:T(8,128)(2,1)S(1)} %get-tuple-element.68), channel_id=1, source_target_pairs={{0,6},{2,4},{4,10},{6,8},{8,14},{10,12},{12,2},{14,0},{1,7},{3,5},... | collective-permute-start | bytes 393224 | tf_op jit(solution)/shard_map/scatter_col/ppermute | solution.py:34
  64.3 3.2 %collective-permute-start.17 = (bf16[512,128]{1,0:T(8,128)(2,1)S(1)}, bf16[512,128]{1,0:T(8,128)(2,1)S(1)}, u32[]{:S(2)}, u32[]{:S(2)}) collective-permute-start(bf16[512,128]{1,0:T(8,128)(2,1)S(1)} %get-tuple-element.72), channel_id=1, source_target_pairs={{0,14},{2,12},{4,2},{6,0},{8,6},{10,4},{12,10},{14,8},{1,15},{3,13... | collective-permute-start | bytes 393224 | tf_op jit(solution)/shard_map/scatter_col/ppermute | solution.py:34
  78.4 2.8 %collective-permute-start.22 = (bf16[512,128]{1,0:T(8,128)(2,1)S(1)}, bf16[512,128]{1,0:T(8,128)(2,1)S(1)}, u32[]{:S(2)}, u32[]{:S(2)}) collective-permute-start(bf16[512,128]{1,0:T(8,128)(2,1)S(1)} %get-tuple-element.76.refs_0_), channel_id=1, source_target_pairs={{8,0},{12,4},{0,8},{4,12},{9,1},{13,5},{1,9},{5,13},{10,2},{14,6},... | collective-permute-start | bytes 393224 | tf_op jit(solution)/shard_map/gather_col/ppermute | solution.py:22
  84.9 3.2 %collective-permute-start.23 = (bf16[512,128]{1,0:T(8,128)(2,1)S(1)}, bf16[512,128]{1,0:T(8,128)(2,1)S(1)}, u32[]{:S(2)}, u32[]{:S(2)}) collective-permute-start(bf16[512,128]{1,0:T(8,128)(2,1)S(1)} %collective-permute-done.19.refs_1_), channel_id=1, source_target_pairs={{8,0},{12,4},{0,8},{4,12},{9,1},{13,5},{1,9},{5,13},{10,2},{14,6},... | collective-permute-start | bytes 393224 | tf_op jit(solution)/shard_map/gather_col/ppermute | solution.py:22
  93.2 3.9 %backward_away.1 = (bf16[1024,128]{1,0:T(8,128)(2,1)S(1)}, bf16[1024,128]{1,0:T(8,128)(2,1)S(1)}, bf16[1024,128]{1,0:T(8,128)(2,1)S(1)}, bf16[1024,128]{1,0:T(8,128)(2,1)S(1)}) custom-call(s32[1]{0:T(128)} %get-tuple-element.121.total_ref, s32[384]{0:T(512)S(1)} %get-tuple-element.115.list_ref, bf16[384,128,128]{2,1,0:T(8,128)(2,1)} %bitcast.8, ...), custom_call_target="tpu_custom_call" | custom-call | flops 1610612736 | bytes 12582912 | tf_op jit(solution)/shard_map/backward_away/pallas_call | solution.py:125
  102.9 2.8 %collective-permute-start.32 = (bf16[1024,128]{1,0:T(8,128)(2,1)S(1)}, bf16[1024,128]{1,0:T(8,128)(2,1)S(1)}, u32[]{:S(2)}, u32[]{:S(2)}) collective-permute-start(bf16[1024,128]{1,0:T(8,128)(2,1)S(1)} %get-tuple-element.86), channel_id=1, source_target_pairs={{0,32},{16,48},{32,0},{48,16},{1,33},{17,49},{33,1},{49,17},{2,34}... | collective-permute-start | bytes 786440 | tf_op jit(solution)/shard_map/scatter_row_away/ppermute | solution.py:26
  106.0 3.9 %backward_near.1 = (bf16[1024,128]{1,0:T(8,128)(2,1)S(1)}, bf16[1024,128]{1,0:T(8,128)(2,1)S(1)}, bf16[1024,128]{1,0:T(8,128)(2,1)S(1)}, bf16[1024,128]{1,0:T(8,128)(2,1)S(1)}) custom-call(s32[1]{0:T(128)} %get-tuple-element.87.total_ref, s32[384]{0:T(512)S(1)} %get-tuple-element.114.list_ref, bf16[384,128,128]{2,1,0:T(8,128)(2,1)} %bitcast.9, ...), custom_call_target="tpu_custom_call" | custom-call | flops 1610612736 | bytes 12582912 | tf_op jit(solution)/shard_map/backward_near/pallas_call | solution.py:125
  111.4 3.4 %collective-permute-done.32.refs_3_ = bf16[1024,128]{1,0:T(8,128)(2,1)S(1)} collective-permute-done((bf16[1024,128]{1,0:T(8,128)(2,1)S(1)}, bf16[1024,128]{1,0:T(8,128)(2,1)S(1)}, u32[]{:S(2)}, u32[]{:S(2)}) %collective-permute-start.32) | collective-permute-done | bytes 262176 | tf_op jit(solution)/shard_map/scatter_row_away/ppermute | solution.py:26
  119.5 2.8 %collective-permute-start.35 = (f32[264,128]{1,0:T(8,128)S(1)}, f32[264,128]{1,0:T(8,128)S(1)}, u32[]{:S(2)}, u32[]{:S(2)}) collective-permute-start(f32[264,128]{1,0:T(8,128)S(1)} %add.101), channel_id=1, source_target_pairs={{0,128},{64,192},{128,0},{192,64},{1,129},{65,193},{129,1},{193,65... | collective-permute-start | bytes 405512 | tf_op jit(solution)/shard_map/weight_grads/ppermute | solution.py:45
  122.3 3.1 %collective-permute-start.39 = (bf16[512,128]{1,0:T(8,128)(2,1)S(1)}, bf16[512,128]{1,0:T(8,128)(2,1)S(1)}, u32[]{:S(2)}, u32[]{:S(2)}) collective-permute-start(bf16[512,128]{1,0:T(8,128)(2,1)S(1)} %get-tuple-element.111), channel_id=1, source_target_pairs={{0,128},{64,192},{128,0},{192,64},{1,129},{65,193},{129,1},{193,65... | collective-permute-start | bytes 393224 | tf_op jit(solution)/shard_map/scatter_row_away/ppermute | solution.py:26
  125.4 3.6 %collective-permute-done.35 = f32[264,128]{1,0:T(8,128)S(1)} collective-permute-done((f32[264,128]{1,0:T(8,128)S(1)}, f32[264,128]{1,0:T(8,128)S(1)}, u32[]{:S(2)}, u32[]{:S(2)}) %collective-permute-start.35) | collective-permute-done | bytes 135200 | tf_op jit(solution)/shard_map/weight_grads/ppermute | solution.py:45
  129.1 5.8 %collective-permute-start.43 = (f32[264,128]{1,0:T(8,128)S(1)}, f32[264,128]{1,0:T(8,128)S(1)}, u32[]{:S(2)}, u32[]{:S(2)}) collective-permute-start(f32[264,128]{1,0:T(8,128)S(1)} %add.102), channel_id=1, source_target_pairs={{12,0},{0,4},{4,8},{8,12},{13,1},{1,5},{5,9},{9,13},{14,2},{2,6},{... | collective-permute-start | bytes 405512 | tf_op jit(solution)/shard_map/weight_grads/ppermute | solution.py:22
  137.0 3.7 %collective-permute-start.40 = (bf16[512,128]{1,0:T(8,128)(2,1)S(1)}, bf16[512,128]{1,0:T(8,128)(2,1)S(1)}, u32[]{:S(2)}, u32[]{:S(2)}) collective-permute-start(bf16[512,128]{1,0:T(8,128)(2,1)S(1)} %get-tuple-element.112), channel_id=1, source_target_pairs={{0,192},{64,0},{128,64},{192,128},{1,193},{65,1},{129,65},{193,129... | collective-permute-start | bytes 393224 | tf_op jit(solution)/shard_map/scatter_row_away/ppermute | solution.py:26
  140.9 3.7 %collective-permute-done.40.refs_3_ = bf16[512,128]{1,0:T(8,128)(2,1)S(1)} collective-permute-done((bf16[512,128]{1,0:T(8,128)(2,1)S(1)}, bf16[512,128]{1,0:T(8,128)(2,1)S(1)}, u32[]{:S(2)}, u32[]{:S(2)}) %collective-permute-start.40) | collective-permute-done | bytes 131104 | tf_op jit(solution)/shard_map/scatter_row_away/ppermute | solution.py:26
  144.6 4.8 %collective-permute-done.38.refs_1_ = bf16[512,128]{1,0:T(8,128)(2,1)S(1)} collective-permute-done((bf16[512,128]{1,0:T(8,128)(2,1)S(1)}, bf16[512,128]{1,0:T(8,128)(2,1)S(1)}, u32[]{:S(2)}, u32[]{:S(2)}) %collective-permute-start.38) | collective-permute-done | bytes 131104 | tf_op jit(solution)/shard_map/scatter_row_near/ppermute | solution.py:26
  (101 shorter events, 56.7 us)
Async XLA Ops:
  0.6 16.3 %collective-permute-start.1 = (bf16[512,128]{1,0:T(8,128)(2,1)}, bf16[512,128]{1,0:T(8,128)(2,1)S(1)}, u32[]{:S(2)}, u32[]{:S(2)}) collective-permute-start(bf16[512,128]{1,0:T(8,128)(2,1)} %param.12), channel_id=1, source_target_pairs={{128,0},{192,64},{0,128},{64,192},{129,1},{193,65},{1,129},{65,193... | collective-permute-start | bytes 393224 | tf_op jit(solution)/shard_map/gather_row/ppermute | solution.py:22
  7.9 12.7 %collective-permute-start = (bf16[512,128]{1,0:T(8,128)(2,1)}, bf16[512,128]{1,0:T(8,128)(2,1)S(1)}, u32[]{:S(2)}, u32[]{:S(2)}) collective-permute-start(bf16[512,128]{1,0:T(8,128)(2,1)} %param.12), channel_id=1, source_target_pairs={{64,0},{128,64},{192,128},{0,192},{65,1},{129,65},{193,129},{1,193... | collective-permute-start | bytes 393224 | tf_op jit(solution)/shard_map/gather_row/ppermute | solution.py:22
  7.9 12.7 %collective-permute-start.2 = (bf16[512,128]{1,0:T(8,128)(2,1)}, bf16[512,128]{1,0:T(8,128)(2,1)S(1)}, u32[]{:S(2)}, u32[]{:S(2)}) collective-permute-start(bf16[512,128]{1,0:T(8,128)(2,1)} %param.12), channel_id=1, source_target_pairs={{192,0},{0,64},{64,128},{128,192},{193,1},{1,65},{65,129},{129,193... | collective-permute-start | bytes 393224 | tf_op jit(solution)/shard_map/gather_row/ppermute | solution.py:22
  20.7 13.4 %collective-permute-start.10 = (bf16[1024,128]{1,0:T(8,128)(2,1)S(1)}, bf16[1024,128]{1,0:T(8,128)(2,1)S(1)}, u32[]{:S(2)}, u32[]{:S(2)}) collective-permute-start(bf16[1024,128]{1,0:T(8,128)(2,1)S(1)} %constant_dynamic-update-slice_fusion.2.refs_0_), channel_id=1, source_target_pairs={{48,0},{0,16},{16,32},{32,48},{49,1},{1,17},{17,33},{33,49},{50,2}... | collective-permute-start | bytes 786440 | tf_op jit(solution)/shard_map/gather_row/ppermute | solution.py:22
  22.3 12.4 %collective-permute-start.9 = (bf16[1024,128]{1,0:T(8,128)(2,1)S(1)}, bf16[1024,128]{1,0:T(8,128)(2,1)S(1)}, u32[]{:S(2)}, u32[]{:S(2)}) collective-permute-start(bf16[1024,128]{1,0:T(8,128)(2,1)S(1)} %constant_dynamic-update-slice_fusion.2.refs_0_), channel_id=1, source_target_pairs={{32,0},{48,16},{0,32},{16,48},{33,1},{49,17},{1,33},{17,49},{34,2}... | collective-permute-start | bytes 786440 | tf_op jit(solution)/shard_map/gather_row/ppermute | solution.py:22
  23.4 18.5 %collective-permute-start.8 = (bf16[1024,128]{1,0:T(8,128)(2,1)S(1)}, bf16[1024,128]{1,0:T(8,128)(2,1)S(1)}, u32[]{:S(2)}, u32[]{:S(2)}) collective-permute-start(bf16[1024,128]{1,0:T(8,128)(2,1)S(1)} %constant_dynamic-update-slice_fusion.2.refs_0_), channel_id=1, source_target_pairs={{16,0},{32,16},{48,32},{0,48},{17,1},{33,17},{49,33},{1,49},{18,2}... | collective-permute-start | bytes 786440 | tf_op jit(solution)/shard_map/gather_row/ppermute | solution.py:22
  25.6 20.1 %collective-permute-start.7 = (bf16[1024,128]{1,0:T(8,128)(2,1)S(1)}, bf16[1024,128]{1,0:T(8,128)(2,1)S(1)}, u32[]{:S(2)}, u32[]{:S(2)}) collective-permute-start(bf16[1024,128]{1,0:T(8,128)(2,1)S(1)} %constant_dynamic-update-slice_fusion.4.refs_0_), channel_id=1, source_target_pairs={{48,0},{0,16},{16,32},{32,48},{49,1},{1,17},{17,33},{33,49},{50,2}... | collective-permute-start | bytes 786440 | tf_op jit(solution)/shard_map/gather_row/ppermute | solution.py:22
  25.7 20.1 %collective-permute-start.6 = (bf16[1024,128]{1,0:T(8,128)(2,1)S(1)}, bf16[1024,128]{1,0:T(8,128)(2,1)S(1)}, u32[]{:S(2)}, u32[]{:S(2)}) collective-permute-start(bf16[1024,128]{1,0:T(8,128)(2,1)S(1)} %constant_dynamic-update-slice_fusion.4.refs_0_), channel_id=1, source_target_pairs={{32,0},{48,16},{0,32},{16,48},{33,1},{49,17},{1,33},{17,49},{34,2}... | collective-permute-start | bytes 786440 | tf_op jit(solution)/shard_map/gather_row/ppermute | solution.py:22
  34.1 13.8 %collective-permute-start.5 = (bf16[1024,128]{1,0:T(8,128)(2,1)S(1)}, bf16[1024,128]{1,0:T(8,128)(2,1)S(1)}, u32[]{:S(2)}, u32[]{:S(2)}) collective-permute-start(bf16[1024,128]{1,0:T(8,128)(2,1)S(1)} %constant_dynamic-update-slice_fusion.4.refs_0_), channel_id=1, source_target_pairs={{16,0},{32,16},{48,32},{0,48},{17,1},{33,17},{49,33},{1,49},{18,2}... | collective-permute-start | bytes 786440 | tf_op jit(solution)/shard_map/gather_row/ppermute | solution.py:22
  52.0 12.3 %collective-permute-start.12 = (bf16[512,128]{1,0:T(8,128)(2,1)S(1)}, bf16[512,128]{1,0:T(8,128)(2,1)S(1)}, u32[]{:S(2)}, u32[]{:S(2)}) collective-permute-start(bf16[512,128]{1,0:T(8,128)(2,1)S(1)} %get-tuple-element.67), channel_id=1, source_target_pairs={{0,4},{2,6},{4,8},{6,10},{8,12},{10,14},{12,0},{14,2},{1,5},{3,7},... | collective-permute-start | bytes 393224 | tf_op jit(solution)/shard_map/scatter_col/ppermute | solution.py:34
  55.1 12.5 %collective-permute-start.13 = (bf16[512,128]{1,0:T(8,128)(2,1)S(1)}, bf16[512,128]{1,0:T(8,128)(2,1)S(1)}, u32[]{:S(2)}, u32[]{:S(2)}) collective-permute-start(bf16[512,128]{1,0:T(8,128)(2,1)S(1)} %get-tuple-element.68), channel_id=1, source_target_pairs={{0,6},{2,4},{4,10},{6,8},{8,14},{10,12},{12,2},{14,0},{1,7},{3,5},... | collective-permute-start | bytes 393224 | tf_op jit(solution)/shard_map/scatter_col/ppermute | solution.py:34
  57.9 11.3 %collective-permute-start.14 = (bf16[512,128]{1,0:T(8,128)(2,1)S(1)}, bf16[512,128]{1,0:T(8,128)(2,1)S(1)}, u32[]{:S(2)}, u32[]{:S(2)}) collective-permute-start(bf16[512,128]{1,0:T(8,128)(2,1)S(1)} %get-tuple-element.69), channel_id=1, source_target_pairs={{0,8},{2,10},{4,12},{6,14},{8,0},{10,2},{12,4},{14,6},{1,9},{3,11}... | collective-permute-start | bytes 393224 | tf_op jit(solution)/shard_map/scatter_col/ppermute | solution.py:34
  58.4 10.8 %collective-permute-start.15 = (bf16[512,128]{1,0:T(8,128)(2,1)S(1)}, bf16[512,128]{1,0:T(8,128)(2,1)S(1)}, u32[]{:S(2)}, u32[]{:S(2)}) collective-permute-start(bf16[512,128]{1,0:T(8,128)(2,1)S(1)} %get-tuple-element.70), channel_id=1, source_target_pairs={{0,10},{2,8},{4,14},{6,12},{8,2},{10,0},{12,6},{14,4},{1,11},{3,9}... | collective-permute-start | bytes 393224 | tf_op jit(solution)/shard_map/scatter_col/ppermute | solution.py:34
  73.9 14.1 %collective-permute-start.26 = (f32[264,128]{1,0:T(8,128)S(1)}, f32[264,128]{1,0:T(8,128)S(1)}, u32[]{:S(2)}, u32[]{:S(2)}) collective-permute-start(f32[264,128]{1,0:T(8,128)S(1)} %get-tuple-element.81), channel_id=1, source_target_pairs={{0,2},{2,0},{1,3},{3,1},{4,6},{6,4},{5,7},{7,5},{8,10},{10,8},{9,1... | collective-permute-start | bytes 405512 | tf_op jit(solution)/shard_map/weight_grads/ppermute | solution.py:45
  78.4 10.9 %collective-permute-start.22 = (bf16[512,128]{1,0:T(8,128)(2,1)S(1)}, bf16[512,128]{1,0:T(8,128)(2,1)S(1)}, u32[]{:S(2)}, u32[]{:S(2)}) collective-permute-start(bf16[512,128]{1,0:T(8,128)(2,1)S(1)} %get-tuple-element.76.refs_0_), channel_id=1, source_target_pairs={{8,0},{12,4},{0,8},{4,12},{9,1},{13,5},{1,9},{5,13},{10,2},{14,6},... | collective-permute-start | bytes 393224 | tf_op jit(solution)/shard_map/gather_col/ppermute | solution.py:22
  101.1 10.3 %collective-permute-start.31 = (bf16[1024,128]{1,0:T(8,128)(2,1)S(1)}, bf16[1024,128]{1,0:T(8,128)(2,1)S(1)}, u32[]{:S(2)}, u32[]{:S(2)}) collective-permute-start(bf16[1024,128]{1,0:T(8,128)(2,1)S(1)} %get-tuple-element.85), channel_id=1, source_target_pairs={{0,48},{16,0},{32,16},{48,32},{1,49},{17,1},{33,17},{49,33},{2,50}... | collective-permute-start | bytes 786440 | tf_op jit(solution)/shard_map/scatter_row_away/ppermute | solution.py:26
  102.9 11.9 %collective-permute-start.32 = (bf16[1024,128]{1,0:T(8,128)(2,1)S(1)}, bf16[1024,128]{1,0:T(8,128)(2,1)S(1)}, u32[]{:S(2)}, u32[]{:S(2)}) collective-permute-start(bf16[1024,128]{1,0:T(8,128)(2,1)S(1)} %get-tuple-element.86), channel_id=1, source_target_pairs={{0,32},{16,48},{32,0},{48,16},{1,33},{17,49},{33,1},{49,17},{2,34}... | collective-permute-start | bytes 786440 | tf_op jit(solution)/shard_map/scatter_row_away/ppermute | solution.py:26
  114.9 14.1 %collective-permute-start.34 = (bf16[1024,128]{1,0:T(8,128)(2,1)S(1)}, bf16[1024,128]{1,0:T(8,128)(2,1)S(1)}, u32[]{:S(2)}, u32[]{:S(2)}) collective-permute-start(bf16[1024,128]{1,0:T(8,128)(2,1)S(1)} %get-tuple-element.104), channel_id=1, source_target_pairs={{0,16},{16,32},{32,48},{48,0},{1,17},{17,33},{33,49},{49,1},{2,18}... | collective-permute-start | bytes 786440 | tf_op jit(solution)/shard_map/scatter_row_near/ppermute | solution.py:26
  115.0 19.8 %collective-permute-start.36 = (bf16[1024,128]{1,0:T(8,128)(2,1)S(1)}, bf16[1024,128]{1,0:T(8,128)(2,1)S(1)}, u32[]{:S(2)}, u32[]{:S(2)}) collective-permute-start(bf16[1024,128]{1,0:T(8,128)(2,1)S(1)} %get-tuple-element.107), channel_id=1, source_target_pairs={{0,48},{16,0},{32,16},{48,32},{1,49},{17,1},{33,17},{49,33},{2,50}... | collective-permute-start | bytes 786440 | tf_op jit(solution)/shard_map/scatter_row_near/ppermute | solution.py:26
  117.0 20.0 %collective-permute-start.37 = (bf16[1024,128]{1,0:T(8,128)(2,1)S(1)}, bf16[1024,128]{1,0:T(8,128)(2,1)S(1)}, u32[]{:S(2)}, u32[]{:S(2)}) collective-permute-start(bf16[1024,128]{1,0:T(8,128)(2,1)S(1)} %get-tuple-element.108), channel_id=1, source_target_pairs={{0,32},{16,48},{32,0},{48,16},{1,33},{17,49},{33,1},{49,17},{2,34}... | collective-permute-start | bytes 786440 | tf_op jit(solution)/shard_map/scatter_row_near/ppermute | solution.py:26
  122.3 18.5 %collective-permute-start.39 = (bf16[512,128]{1,0:T(8,128)(2,1)S(1)}, bf16[512,128]{1,0:T(8,128)(2,1)S(1)}, u32[]{:S(2)}, u32[]{:S(2)}) collective-permute-start(bf16[512,128]{1,0:T(8,128)(2,1)S(1)} %get-tuple-element.111), channel_id=1, source_target_pairs={{0,128},{64,192},{128,0},{192,64},{1,129},{65,193},{129,1},{193,65... | collective-permute-start | bytes 393224 | tf_op jit(solution)/shard_map/scatter_row_away/ppermute | solution.py:26
  129.1 21.1 %collective-permute-start.43 = (f32[264,128]{1,0:T(8,128)S(1)}, f32[264,128]{1,0:T(8,128)S(1)}, u32[]{:S(2)}, u32[]{:S(2)}) collective-permute-start(f32[264,128]{1,0:T(8,128)S(1)} %add.102), channel_id=1, source_target_pairs={{12,0},{0,4},{4,8},{8,12},{13,1},{1,5},{5,9},{9,13},{14,2},{2,6},{... | collective-permute-start | bytes 405512 | tf_op jit(solution)/shard_map/weight_grads/ppermute | solution.py:22
  134.8 15.3 %collective-permute-start.42 = (f32[264,128]{1,0:T(8,128)S(1)}, f32[264,128]{1,0:T(8,128)S(1)}, u32[]{:S(2)}, u32[]{:S(2)}) collective-permute-start(f32[264,128]{1,0:T(8,128)S(1)} %add.102), channel_id=1, source_target_pairs={{4,0},{8,4},{12,8},{0,12},{5,1},{9,5},{13,9},{1,13},{6,2},{10,6},{... | collective-permute-start | bytes 405512 | tf_op jit(solution)/shard_map/weight_grads/ppermute | solution.py:22
  134.8 15.3 %collective-permute-start.41 = (f32[264,128]{1,0:T(8,128)S(1)}, f32[264,128]{1,0:T(8,128)S(1)}, u32[]{:S(2)}, u32[]{:S(2)}) collective-permute-start(f32[264,128]{1,0:T(8,128)S(1)} %add.102), channel_id=1, source_target_pairs={{8,0},{12,4},{0,8},{4,12},{9,1},{13,5},{1,9},{5,13},{10,2},{14,6},... | collective-permute-start | bytes 405512 | tf_op jit(solution)/shard_map/weight_grads/ppermute | solution.py:22
  (20 other events, 148.4 us)
